TPU v7x, 512 devices: a whole 4x8x8 slice. The times are simulated.
512 devices in a mesh: dap: 128 (over y, z_hi, x, core), dp: 4 (over z_lo).
Axes of the slice: x: 4, y: 8, z: 8 (z_hi: 2, z_lo: 4; z = z_hi * 4 + z_lo), core: 2. Of those that a mesh axis runs over, the one named last changes fastest.
Arguments:
- lineup_embedding: bfloat16 [512, 128, 256], P(('dp', 'dap')), parts along dimension 0, may hold values from -6 to 6
- occupancy_flags: int32 [512, 128], P(('dp', 'dap')), parts along dimension 0, may hold values 0 or 1
- couple_embedding: bfloat16 [512, 128, 128], P(('dp', 'dap')), parts along dimension 0, may hold values from -6 to 6
- couple_offset_matrix: bfloat16 [128, 8], replicated
- horizontal_attend_matrices: bfloat16 [256, 1024], replicated, may hold values from -0.375 to 0.375
- horizontal_final_matrix: bfloat16 [256, 256], replicated, may hold values from -0.375 to 0.375
- vertical_attend_matrices: bfloat16 [256, 1024], replicated, may hold values from -0.375 to 0.375
- vertical_final_matrix: bfloat16 [256, 256], replicated, may hold values from -0.375 to 0.375
- tensor_first_matrix: bfloat16 [256, 32], replicated, may hold values from -1.5 to 1.5
- tensor_second_matrix: bfloat16 [256, 32], replicated, may hold values from -1.5 to 1.5
- tensor_final_matrix: bfloat16 [1024, 128], replicated, may hold values from -0.1875 to 0.1875
Outputs:
- alignment_updated: bfloat16 [512, 128, 256], P('dp', 'dap'), parts along dimension 0
- pair_updated: bfloat16 [512, 128, 128], P(('dp', 'dap')), parts along dimension 0
There are 4 independent parts, one for each index of `dp`. A program takes and returns all parts, laid end to end along the dimension named above; an argument that names none is the same for every part. Nothing has to cross between parts.
All inputs are finite; a program needn't handle non-finite values. No bound on the sum of `occupancy_flags` on one device may be relied on, other than what follows from the above.
Results may differ from a plain program's by a relative error of at most 0.015.
The roundings to bfloat16 on the way count: a program that leaves them out, or rounds other values in their place, can miss the bound.
Values may be sent and summed in bfloat16 or wider, within the bound.
A program may use at most 64 MiB of HBM per device.

v0:
```python
import jax
import jax.numpy as jnp
from jax import lax
from jax.sharding import PartitionSpec as P

FOCUS_GROUPS = 8
GROUP_FEATURES = 32
TENSOR_FEATURES = 32


epsilon = 1e-05
masked = 1000000000.0


def standardize_features(values):
    wide = values.astype(jnp.float32)
    average = jnp.mean(wide, axis=-1, keepdims=True)
    centred = wide - average
    variance = jnp.mean(centred * centred, axis=-1, keepdims=True)
    return (centred * lax.rsqrt(variance + epsilon)).astype(jnp.bfloat16)


def soft_rows(scores):
    row_max = jnp.max(scores, axis=-1, keepdims=True)
    expo = jnp.exp(scores - row_max)
    return (expo / jnp.sum(expo, axis=-1, keepdims=True)).astype(jnp.bfloat16)


def split_heads(mapped_features, width):
    lead = mapped_features.shape[:-1]
    question_vectors = (
        (mapped_features[..., :width] * GROUP_FEATURES ** (-0.5))
        .astype(jnp.bfloat16)
        .reshape(lead + (FOCUS_GROUPS, GROUP_FEATURES))
    )
    lookup_vectors = (
        mapped_features[..., width : 2 * width]
        .astype(jnp.bfloat16)
        .reshape(lead + (FOCUS_GROUPS, GROUP_FEATURES))
    )
    content_vectors = (
        mapped_features[..., 2 * width : 3 * width]
        .astype(jnp.bfloat16)
        .reshape(lead + (FOCUS_GROUPS, GROUP_FEATURES))
    )
    sigmoid_factors = jax.nn.sigmoid(mapped_features[..., 3 * width :])
    return (question_vectors, lookup_vectors, content_vectors, sigmoid_factors)


def per_device(
    lineup_embedding,
    occupancy_flags,
    couple_embedding,
    couple_offset_matrix,
    horizontal_attend_matrices,
    horizontal_final_matrix,
    vertical_attend_matrices,
    vertical_final_matrix,
    tensor_first_matrix,
    tensor_second_matrix,
    tensor_final_matrix,
):
    present_mask = occupancy_flags.astype(jnp.float32)
    pair_normed = standardize_features(couple_embedding)
    local_bias = jnp.einsum(
        "ijc,ch->hij", pair_normed, couple_offset_matrix, preferred_element_type=jnp.float32
    ).astype(jnp.bfloat16)
    standardized_source = standardize_features(lineup_embedding)
    seqs_here, residues, width = standardized_source.shape
    mapped_features = jnp.einsum(
        "bnc,ce->bne",
        standardized_source,
        horizontal_attend_matrices,
        preferred_element_type=jnp.float32,
    )
    question_vectors, lookup_vectors, content_vectors, sigmoid_factors = split_heads(
        mapped_features, width
    )
    key_bias = (present_mask - 1.0) * masked
    full_bias = lax.all_gather(local_bias, "dap", axis=1, tiled=True)
    extent_count = full_bias.shape[1]
    extra = full_bias.astype(jnp.float32)

    def one_sequence(items):
        query_seq, key_seq, value_seq, gate_seq, bias_seq = items
        scores = jnp.einsum("qhd,khd->hqk", query_seq, key_seq, preferred_element_type=jnp.float32)
        scores = scores + bias_seq[None, None, :] + extra
        attention_probabilities = soft_rows(scores)
        blended_values = jnp.einsum(
            "fsg,gfe->sfe", attention_probabilities, value_seq, preferred_element_type=jnp.float32
        ).reshape(extent_count, width)
        gated = (gate_seq * blended_values).astype(jnp.bfloat16)
        return jnp.dot(gated, horizontal_final_matrix, preferred_element_type=jnp.float32)

    horizontal_increment = lax.map(
        one_sequence, (question_vectors, lookup_vectors, content_vectors, sigmoid_factors, key_bias)
    )
    lineup_chain_slices = (lineup_embedding.astype(jnp.float32) + horizontal_increment).astype(
        jnp.bfloat16
    )
    column_entries, column_live = (
        lax.all_to_all(lineup_chain_slices, "dap", split_axis=1, concat_axis=0, tiled=True),
        lax.all_to_all(
            present_mask.astype(jnp.bfloat16), "dap", split_axis=1, concat_axis=0, tiled=True
        ),
    )
    seqs_all, residues_here = column_live.shape
    col_normed = standardize_features(column_entries)
    col_projected = jnp.einsum(
        "src,ce->sre", col_normed, vertical_attend_matrices, preferred_element_type=jnp.float32
    )
    col_queries, col_keys, col_values, col_gates = split_heads(col_projected, width)
    live_cols = column_live.astype(jnp.float32)
    col_scores = jnp.einsum(
        "qrhd,krhd->rhqk", col_queries, col_keys, preferred_element_type=jnp.float32
    )
    col_scores = col_scores + ((live_cols.T - 1.0) * masked)[:, None, None, :]
    col_soft = soft_rows(col_scores)
    col_mixed = jnp.einsum(
        "rhqk,krhd->qrhd", col_soft, col_values, preferred_element_type=jnp.float32
    ).reshape(seqs_all, residues_here, width)
    col_gated = (col_gates * col_mixed).astype(jnp.bfloat16)
    column_update = jnp.einsum(
        "src,ce->sre", col_gated, vertical_final_matrix, preferred_element_type=jnp.float32
    )
    alignment_updated = (column_entries.astype(jnp.float32) + column_update).astype(jnp.bfloat16)
    outer_normalized = standardize_features(alignment_updated)
    live_rows = live_cols.T
    left = (
        jnp.einsum(
            "src,cd->rds", outer_normalized, tensor_first_matrix, preferred_element_type=jnp.float32
        )
        * live_rows[:, None, :]
    ).astype(jnp.bfloat16)
    second_mapped = (
        jnp.einsum(
            "src,cd->rds",
            outer_normalized,
            tensor_second_matrix,
            preferred_element_type=jnp.float32,
        )
        * live_rows[:, None, :]
    ).astype(jnp.bfloat16)
    right_rows = second_mapped.reshape(residues_here, TENSOR_FEATURES * seqs_all)
    mask_rows = column_live.T
    left_flat = left.reshape(residues_here * TENSOR_FEATURES, seqs_all)
    right_all, mask_all = (
        lax.all_gather(right_rows, "dap", axis=0, tiled=True),
        lax.all_gather(mask_rows, "dap", axis=0, tiled=True),
    )
    outer_extent_count = right_all.shape[0]
    second_reshaped = right_all.reshape(outer_extent_count * TENSOR_FEATURES, seqs_all)
    products = lax.dot_general(
        left_flat, second_reshaped, (((1,), (1,)), ((), ())), preferred_element_type=jnp.float32
    )
    products = products.reshape(
        residues_here, TENSOR_FEATURES, outer_extent_count, TENSOR_FEATURES
    ).transpose(0, 2, 1, 3)
    products = products.reshape(
        residues_here, outer_extent_count, TENSOR_FEATURES * TENSOR_FEATURES
    ).astype(jnp.bfloat16)
    outer_proj = jnp.einsum(
        "rjf,fz->rjz", products, tensor_final_matrix, preferred_element_type=jnp.float32
    )
    counts = lax.dot_general(
        mask_rows, mask_all, (((1,), (1,)), ((), ())), preferred_element_type=jnp.float32
    )
    update = outer_proj / jnp.maximum(counts, 1.0)[:, :, None]
    pair_updated = (couple_embedding.astype(jnp.float32) + update).astype(jnp.bfloat16)
    return (alignment_updated, pair_updated)


def solution(mesh):
    return jax.shard_map(
        per_device,
        mesh=mesh,
        in_specs=(
            P(("dp", "dap"), None, None),
            P(("dp", "dap"), None),
            P(("dp", "dap"), None, None),
            P(),
            P(),
            P(),
            P(),
            P(),
            P(),
            P(),
            P(),
        ),
        out_specs=(P("dp", "dap", None), P(("dp", "dap"), None, None)),
        check_vma=False,
    )
```

profile of v0, /device:TPU:1, one launch (start us, length us, event | category | flops | bytes accessed | tf_op | source)
XLA Modules:
  0.0 515.5 jit_solution(6095990889009458919)
XLA Ops:
  7.2 0.7 convert_bitcast_fusion.3
  7.9 0.8 copy.66
  8.7 20.8 %all-to-all-start.1 = ((bf16[1,128,1]{2,0,1:T(2,128)(2,1)}), bf16[1,128,1]{2,0,1:T(2,128)(2,1)S(1)}, u32[]{:S(2)}, u32[]{:S(2)}) async-start(bf16[1,128,1]{2,0,1:T(2,128)(2,1)} %copy.66), calls=%async_computation.1 | async-start | bytes 131072 | tf_op jit(solution)/shard_map/all_to_all | solution.py:103
  29.5 0.7 multiply_bitcast_fusion
  30.2 0.9 convert_reduce_fusion.1
  31.1 1.0 fusion.27
  32.2 0.9 convert_reduce_fusion.3
  33.1 0.9 fusion.51
  34.0 1.0 fusion.18
  35.0 224.6 %all-gather = bf16[8,16384]{1,0:T(8,128)(2,1)S(1)} all-gather(bf16[8,128]{1,0:T(8,128)(2,1)S(1)} %fusion.18), channel_id=2, replica_groups=mesh['dap'=128,'dp'=4] {'dap'}, dimensions={1}, use_global_device_ids=true | all-gather | bytes 264192 | tf_op jit(solution)/shard_map/all_gather | solution.py:80
  259.8 0.2 copy.58
  260.0 0.3 fusion.81
  260.7 0.3 fusion.6
  261.1 0.2 fusion.20
  261.9 0.5 broadcast.200
  262.4 1.0 reduce.17
  263.4 0.7 reshape.331
  264.1 5.6 %all-to-all-start = ((bf16[128,2,128]{2,1,0:T(2,128)(2,1)}), bf16[128,2,128]{2,1,0:T(2,128)(2,1)S(1)}, u32[]{:S(2)}, u32[]{:S(2)}) async-start(bf16[128,2,128]{2,1,0:T(2,128)(2,1)} %reshape.331), calls=%async_computation | async-start | bytes 131072 | tf_op jit(solution)/shard_map/all_to_all | solution.py:102
  269.7 1.0 reduce.15
  270.8 13.3 %all-to-all-done = bf16[128,2,128]{2,1,0:T(2,128)(2,1)S(1)} async-done(((bf16[128,2,128]{2,1,0:T(2,128)(2,1)}), bf16[128,2,128]{2,1,0:T(2,128)(2,1)S(1)}, u32[]{:S(2)}, u32[]{:S(2)}) %all-to-all-start) | async-done | bytes 65568 | tf_op jit(solution)/shard_map/all_to_all | solution.py:102
  284.3 0.2 fusion.35
  284.5 0.3 fusion.83
  285.0 0.4 fusion.84
  285.4 0.3 convolution_add_fusion
  285.8 0.2 fusion.21
  286.2 0.3 convert_reduce_fusion.2
  286.7 0.2 fusion.16
  286.9 0.6 reshape.321
  287.6 214.2 %all-gather.1 = bf16[128,128,1]{1,2,0:T(2,128)(2,1)S(1)} all-gather(bf16[1,128,1]{1,2,0:T(2,128)(2,1)S(1)} %copy.72), channel_id=3, replica_groups=mesh['dap'=128,'dp'=4] {'dap'}, dimensions={0}, use_global_device_ids=true | all-gather | bytes 33024 | tf_op jit(solution)/shard_map/all_gather | solution.py:149
  502.0 5.1 copy.69
  507.1 0.5 fusion.7
  507.7 0.9 fusion.13
  (57 shorter events, 2.4 us)
Async XLA Ops:
  7.2 252.8 %copy-start = (bf16[256,1024]{1,0:T(8,128)(2,1)S(1)}, bf16[256,1024]{1,0:T(8,128)(2,1)}, u32[]{:S(2)}) copy-start(bf16[256,1024]{1,0:T(8,128)(2,1)} %param.15) | copy-start | bytes 1572868
  7.2 252.8 %copy-start.1 = (bf16[1,128,256]{2,1,0:T(8,128)(2,1)S(1)}, bf16[1,128,256]{2,1,0:T(8,128)(2,1)}, u32[]{:S(2)}) copy-start(bf16[1,128,256]{2,1,0:T(8,128)(2,1)} %param.11) | copy-start | bytes 196612
  8.7 255.4 %all-to-all-start.1 = ((bf16[1,128,1]{2,0,1:T(2,128)(2,1)}), bf16[1,128,1]{2,0,1:T(2,128)(2,1)S(1)}, u32[]{:S(2)}, u32[]{:S(2)}) async-start(bf16[1,128,1]{2,0,1:T(2,128)(2,1)} %copy.66), calls=%async_computation.1 | async-start | bytes 131072 | tf_op jit(solution)/shard_map/all_to_all | solution.py:103
  260.7 0.9 copy-start.7
  261.1 23.4 %copy-start.2 = (bf16[256,1024]{1,0:T(8,128)(2,1)S(1)}, bf16[256,1024]{1,0:T(8,128)(2,1)}, u32[]{:S(2)}) copy-start(bf16[256,1024]{1,0:T(8,128)(2,1)} %param.17) | copy-start | bytes 1572868
  264.1 20.1 %all-to-all-start = ((bf16[128,2,128]{2,1,0:T(2,128)(2,1)}), bf16[128,2,128]{2,1,0:T(2,128)(2,1)S(1)}, u32[]{:S(2)}, u32[]{:S(2)}) async-start(bf16[128,2,128]{2,1,0:T(2,128)(2,1)} %reshape.331), calls=%async_computation | async-start | bytes 131072 | tf_op jit(solution)/shard_map/all_to_all | solution.py:102
  269.7 232.3 %all-gather.5.cloned.1.call-start = ((), (), s32[]{:S(2)}) async-start(), calls=%async_computation.2 | async-start | bytes 2113536 | tf_op jit(solution)/shard_map/all_gather | solution.py:148
  284.9 1.3 copy-start.8
  285.4 1.3 copy-start.9
  286.2 220.9 %copy-start.5 = (bf16[256,32]{0,1:T(8,128)(2,1)S(1)}, bf16[256,32]{0,1:T(8,128)(2,1)}, u32[]{:S(2)}) copy-start(bf16[256,32]{0,1:T(8,128)(2,1)} %param.19) | copy-start | bytes 49156
  286.4 221.1 %copy-start.3 = (bf16[128,256]{1,0:T(8,128)(2,1)}, bf16[128,256]{1,0:T(8,128)(2,1)S(1)}, u32[]{:S(2)}) copy-start(bf16[128,256]{1,0:T(8,128)(2,1)S(1)} %get-tuple-element.40) | copy-start | bytes 196612
  502.0 5.8 %copy-start.4 = (bf16[1,128,128]{2,1,0:T(8,128)(2,1)S(1)}, bf16[1,128,128]{2,1,0:T(8,128)(2,1)}, u32[]{:S(2)}) copy-start(bf16[1,128,128]{2,1,0:T(8,128)(2,1)} %param.13) | copy-start | bytes 98308
  502.0 5.8 %copy-start.6 = (bf16[1024,128]{1,0:T(8,128)(2,1)S(1)}, bf16[1024,128]{1,0:T(8,128)(2,1)}, u32[]{:S(2)}) copy-start(bf16[1024,128]{1,0:T(8,128)(2,1)} %param.21) | copy-start | bytes 786436
Sparse Core Ops, SparseCore 0:
  287.7 123.6 all-gather.4
where the time goes:
time: 516 us; the launch traced here: 515 us
  blocking collectives  439 us (85%)
  starting transfers between devices  26.5 us (5%)
  between operations  14.5 us (3%)
  waiting for transfers between devices  13.4 us (3%)
  local copies, waits for them, and re-layouts  9.35 us (2%)
  other arithmetic  7.88 us (2%)
    all_gather x1, blocking collectives, per_device(): full_bias = lax.all_gather(local_bias, 'dap', axis=1, tiled=True)  225 us
    all_gather x1, blocking collectives, per_device(): lax.all_gather(mask_rows, 'dap', axis=0, tiled=True)  214 us
    all_to_all x1, starting transfers between devices, per_device(): lax.all_to_all(present_mask.astype(jnp.bfloat16), 'dap', split_axis=1, co...  20.8 us
    all_to_all x1, waiting for transfers between devices, per_device(): lax.all_to_all(lineup_chain_slices, 'dap', split_axis=1, concat_axis=0, t...  13.3 us
  transfers between devices with their start and end apart: 3, of which 1 were waited for; matrix products, arithmetic and copies ran while one was open for 2% of the time, Pallas kernels for 0%

commit v1 on v0

v1 whole, which is shorter than its diff:
```python
import functools

import jax
import jax.numpy as jnp
from jax import lax
from jax.experimental import pallas as pl
from jax.experimental.pallas import tpu as pltpu
from jax.sharding import PartitionSpec as P

HEADS = 8
HEAD_DIM = 32
WIDTH = 256
PAIR = 128
OUTER = 32
LANES = 128
EPS = 1e-5
MASKED = 1e9
NB = 8

F32 = jnp.float32
BF16 = jnp.bfloat16
MESH = pl.DeviceIdType.MESH


def normed(x):
    average = jnp.mean(x, axis=-1, keepdims=True)
    centred = x - average
    variance = jnp.mean(centred * centred, axis=-1, keepdims=True)
    return (centred * lax.rsqrt(variance + EPS)).astype(BF16)


def dot(a, b):
    return jnp.dot(a, b, preferred_element_type=F32)


def dot_nt(a, b):
    return lax.dot_general(a, b, (((1,), (1,)), ((), ())), preferred_element_type=F32)


def iota(shape, axis):
    return lax.broadcasted_iota(jnp.int32, shape, axis)


def head_mask(rows_per_head):
    shape = (HEADS * rows_per_head, WIDTH)
    return iota(shape, 0) // rows_per_head == iota(shape, 1) // HEAD_DIM


def kernel(
    na,
    lineup,
    flags,
    couple,
    offset_t,
    w_row,
    w_row_out,
    w_col,
    w_col_out,
    w_outer_t,
    w_final,
    align_out,
    pair_out,
    lineup_v,
    flags_v,
    couple_v,
    offset_v,
    w_row_v,
    w_row_out_v,
    w_col_v,
    w_col_out_v,
    w_outer_v,
    w_final_v,
    wide,
    bias_buf,
    bias_wide,
    small_send,
    small_buf,
    live_send,
    live_buf,
    x_buf,
    gated_buf,
    rows_wide,
    rows_send,
    rows_buf,
    left_buf,
    right_buf,
    products,
    final_rep,
    update_send,
    update_buf,
    align_v,
    pair_v,
    in_sems,
    out_sems,
    send_sems,
    recv_sems,
    x_sems,
):
    n = na * NB
    me = lax.axis_index("dap")
    a, b = me // NB, me % NB

    def b_mate(r):
        return (b + r) % NB

    def a_mate(r):
        return (a + r) % na

    barrier = pltpu.get_barrier_semaphore()
    for r in range(1, NB):
        pl.semaphore_signal(
            barrier, inc=1, device_id={"dap": a * NB + b_mate(r)}, device_id_type=MESH
        )
    for r in range(1, na):
        pl.semaphore_signal(
            barrier, inc=1, device_id={"dap": a_mate(r) * NB + b}, device_id_type=MESH
        )

    pairs = (
        (lineup.at[0], lineup_v),
        (flags, flags_v),
        (couple.at[0], couple_v),
        (offset_t, offset_v),
        (w_row, w_row_v),
        (w_row_out, w_row_out_v),
        (w_col, w_col_v),
        (w_col_out, w_col_out_v),
        (w_outer_t, w_outer_v),
        (w_final, w_final_v),
    )
    loads = [pltpu.make_async_copy(src, dst, in_sems.at[k]) for k, (src, dst) in enumerate(pairs)]
    for load in loads:
        load.start()

    def send(src, dst, phase, device):
        copy = pltpu.make_async_remote_copy(
            src_ref=src,
            dst_ref=dst,
            send_sem=send_sems.at[phase],
            recv_sem=recv_sems.at[phase],
            device_id={"dap": device},
            device_id_type=MESH,
        )
        copy.start()

    def batch(ref, phase):
        return pltpu.make_async_remote_copy(
            src_ref=ref,
            dst_ref=ref,
            send_sem=send_sems.at[phase],
            recv_sem=recv_sems.at[phase],
            device_id={"dap": a * NB + b_mate(1)},
            device_id_type=MESH,
        )

    loads[0].wait()
    x = lineup_v[...].astype(F32)
    wide[0] = x[:, :LANES]
    wide[1] = x[:, LANES:]
    raw = jnp.concatenate(
        [
            jnp.concatenate([wide[h, pl.ds(k, na, stride=NB), :] for k in range(NB)], axis=0)
            for h in range(2)
        ],
        axis=1,
    )
    x_norm = normed(raw)
    x_buf[b] = x_norm

    loads[1].wait()
    order = (iota((n, n), 1) == (iota((n, n), 0) % na) * NB + iota((n, n), 0) // na).astype(BF16)
    live = dot_nt(
        jnp.broadcast_to(flags_v[...], (2 * NB, n)).astype(F32).astype(BF16), order
    )
    raw16 = raw.astype(BF16)
    for k in range(NB):
        rows = slice(k * na, (k + 1) * na)
        small_send[k] = jnp.concatenate(
            [raw16[rows], x_norm[rows], jnp.broadcast_to(live[:1], (na, n)).astype(BF16)], axis=1
        )

    loads[2].wait()
    loads[3].wait()
    wide[0, :, :PAIR] = couple_v[...].astype(F32)
    pair = jnp.concatenate([wide[0, pl.ds(k, na, stride=NB), :] for k in range(NB)], axis=0)
    bias = dot_nt(offset_v[...], normed(pair))
    bias_buf[a] = jnp.concatenate([bias, jnp.zeros_like(bias)], axis=0).astype(BF16)

    pl.semaphore_wait(barrier, NB + na - 2)

    for r in range(1, NB):
        mate = b_mate(r)
        send(small_send.at[mate], small_buf.at[b], 0, a * NB + mate)
    for r in range(1, na):
        send(bias_buf.at[a], bias_buf.at[a], 1, a_mate(r) * NB + b)
    for r in range(1, NB):
        pltpu.make_async_remote_copy(
            src_ref=x_buf.at[b],
            dst_ref=x_buf.at[b],
            send_sem=send_sems.at[2],
            recv_sem=x_sems.at[r],
            device_id={"dap": a * NB + b_mate(r)},
            device_id_type=MESH,
        ).start()
    small_buf[b] = small_send[b]

    loads[9].wait()
    products[...] = w_final_v[...].astype(F32)
    for d in range(OUTER):
        part = products[pl.ds(d, OUTER, stride=OUTER), :].astype(BF16)
        for k in range(4):
            final_rep[pl.ds((d * 4 + k) * OUTER, OUTER), :] = part

    batch(small_buf.at[pl.ds(0, NB - 1)], 0).wait_recv()
    small = small_buf[...]
    live8 = small[:, :8, 2 * WIDTH :].astype(F32)[:, 0, :]
    live_send[...] = jnp.concatenate([live8, live8], axis=0).astype(BF16)
    for r in range(1, na):
        send(live_send, live_buf.at[a], 3, a_mate(r) * NB + b)
    live_buf[a] = live_send[...]

    loads[4].wait()
    queries_in = small[:, :, WIDTH : 2 * WIDTH].reshape(NB * na, WIDTH)
    queries = (dot(queries_in, w_row_v[:, :WIDTH]) * HEAD_DIM**-0.5).astype(BF16)
    gates = jax.nn.sigmoid(dot(queries_in, w_row_v[:, 3 * WIDTH :]))
    rows_wide[0] = gates[:, :LANES]
    rows_wide[1] = gates[:, LANES:]
    gated_buf[...] = queries.reshape(NB, na, WIDTH)

    batch(bias_buf.at[pl.ds(0, na - 1)], 1).wait_recv()
    bias_wide[...] = bias_buf[...].astype(F32).reshape(na * 16, n)
    score_bias = jnp.concatenate(
        [bias_wide[pl.ds(h, na, stride=16), :] for h in range(HEADS)], axis=0
    )
    own_head = head_mask(na)
    lane_head = iota((na, WIDTH), 1) // HEAD_DIM
    ones = jnp.ones((n, LANES), BF16)

    for r in range(NB):
        seq = (b + NB - r) % NB
        if r > 0:
            pltpu.make_async_remote_copy(
                src_ref=x_buf.at[seq],
                dst_ref=x_buf.at[seq],
                send_sem=send_sems.at[2],
                recv_sem=x_sems.at[r],
                device_id={"dap": a * NB + b_mate(1)},
                device_id_type=MESH,
            ).wait_recv()
        kv = dot(x_buf[seq], w_row_v[:, WIDTH : 3 * WIDTH]).astype(BF16)
        keys, values = kv[:, :WIDTH], kv[:, WIDTH:]
        query = gated_buf[seq]
        spread = jnp.where(own_head, jnp.concatenate([query] * HEADS, axis=0), 0)
        scores = dot_nt(spread, keys)
        key_live = small_buf[seq, :, 2 * WIDTH :].astype(F32)[:1]
        scores = scores + (key_live - 1.0) * MASKED + score_bias
        expo = jnp.exp(scores - jnp.max(scores, axis=-1, keepdims=True)).astype(BF16)
        mixed = dot(expo, values)
        total = dot(expo, ones)
        top, bottom = mixed[:na], jnp.concatenate([total[:na]] * 2, axis=1)
        for h in range(1, HEADS):
            rows = slice(h * na, (h + 1) * na)
            top = jnp.where(lane_head == h, mixed[rows], top)
            bottom = jnp.where(
                lane_head == h, jnp.concatenate([total[rows]] * 2, axis=1), bottom
            )
        at = pl.ds(pl.multiple_of(seq * na, na), na)
        gate = jnp.concatenate([rows_wide[0, at, :], rows_wide[1, at, :]], axis=1)
        gated_buf[seq] = (gate * (top / bottom)).astype(BF16)

    loads[5].wait()
    grown = dot(gated_buf[...].reshape(NB * na, WIDTH), w_row_out_v[...])
    grown = small_buf[:, :, :WIDTH].reshape(NB * na, WIDTH).astype(F32) + grown
    rows_wide[0] = grown[:, :LANES]
    rows_wide[1] = grown[:, LANES:]
    for k in range(na):
        rows_send[k] = jnp.concatenate(
            [rows_wide[h, pl.ds(k, NB, stride=na), :] for h in range(2)], axis=0
        ).astype(BF16)
    for r in range(1, na):
        mate = a_mate(r)
        send(rows_send.at[mate], rows_buf.at[a], 4, mate * NB + b)
    rows_buf[a] = rows_send[a]

    batch(live_buf.at[pl.ds(0, na - 1)], 3).wait_recv()
    live_all = live_buf[...].astype(F32)[:, :NB].reshape(n, n).astype(BF16)
    own = (iota((16, n), 1) == b * na + a).astype(BF16)
    own_live = dot_nt(own, live_all)[:1]
    pick = (NB * na, n)
    pick_i = (iota(pick, 1) == (iota(pick, 0) // na) * na + a).astype(BF16)
    pick_j = (iota(pick, 1) == iota(pick, 0) % na + b * na).astype(BF16)
    counts = jnp.sum(
        dot_nt(pick_i, live_all) * dot_nt(pick_j, live_all), axis=-1, keepdims=True
    )
    counts = jnp.maximum(counts, 1.0)
    col_head = iota((n, WIDTH), 1) // HEAD_DIM
    ones_bd = (
        iota((HEADS * n, WIDTH), 0) // n == iota((HEADS * n, WIDTH), 1) // HEAD_DIM
    ).astype(BF16)
    loads[6].wait()
    loads[7].wait()
    loads[8].wait()

    batch(rows_buf.at[pl.ds(0, na - 1)], 4).wait_recv()
    arrived = rows_buf[...].astype(F32)
    column = jnp.concatenate(
        [arrived[:, :NB].reshape(n, LANES), arrived[:, NB:].reshape(n, LANES)], axis=1
    )
    mapped = dot(normed(column), w_col_v[...])
    queries = (mapped[:, :WIDTH] * HEAD_DIM**-0.5).astype(BF16)
    keys = mapped[:, WIDTH : 2 * WIDTH].astype(BF16)
    values = mapped[:, 2 * WIDTH : 3 * WIDTH].astype(BF16)
    key_bias = (own_live - 1.0) * MASKED
    expos, spread_values = [], []
    for h in range(HEADS):
        scores = dot_nt(jnp.where(col_head == h, queries, 0), keys) + key_bias
        expos.append(jnp.exp(scores - jnp.max(scores, axis=-1, keepdims=True)).astype(BF16))
        spread_values.append(jnp.where(col_head == h, values, 0))
    expo = jnp.concatenate(expos, axis=1)
    mixed = dot(expo, jnp.concatenate(spread_values, axis=0)) / dot(expo, ones_bd)
    gated = (jax.nn.sigmoid(mapped[:, 3 * WIDTH :]) * mixed).astype(BF16)
    updated = (column + dot(gated, w_col_out_v[...])).astype(BF16)
    align_v[...] = updated
    align_copy = pltpu.make_async_copy(align_v, align_out, out_sems.at[0])
    align_copy.start()

    outer = (dot_nt(w_outer_v[...], normed(updated.astype(F32))) * own_live).astype(BF16)
    left_buf[b] = outer[:OUTER]
    right_buf[a] = outer[OUTER:]
    for r in range(1, na):
        send(right_buf.at[a], right_buf.at[a], 6, a_mate(r) * NB + b)
    for r in range(1, NB):
        send(left_buf.at[b], left_buf.at[b], 5, a * NB + b_mate(r))
    batch(left_buf.at[pl.ds(0, NB - 1)], 5).wait_recv()
    batch(right_buf.at[pl.ds(0, na - 1)], 6).wait_recv()
    lefts = left_buf[...].reshape(NB * OUTER, n)
    rights = right_buf[...].reshape(na * OUTER, n)
    product = dot_nt(rights, lefts)
    depth = na * OUTER
    products[pl.ds(0, depth), :] = product[:, :LANES]
    products[pl.ds(depth, depth), :] = product[:, LANES:]
    quarter = iota((na, LANES), 1) // OUTER
    step = 8
    total = None
    for first in range(0, OUTER, step):
        slabs = []
        for d in range(first, first + step):
            tiles = [
                products[pl.ds(t * depth + d, na, stride=OUTER), :].astype(BF16) for t in range(2)
            ]
            slabs.append(
                jnp.concatenate(
                    [jnp.where(quarter == i % 4, tiles[i // 4], 0) for i in range(NB)], axis=0
                )
            )
        term = dot(
            jnp.concatenate(slabs, axis=1),
            final_rep[pl.ds(first * LANES, step * LANES), :],
        )
        total = term if total is None else total + term
    update_send[...] = (total / counts).reshape(NB, na, PAIR)
    for r in range(1, NB):
        mate = b_mate(r)
        send(update_send.at[mate], update_buf.at[pl.ds(b * na, na)], 7, a * NB + mate)
    update_buf[pl.ds(b * na, na)] = update_send[b]
    batch(update_send.at[pl.ds(0, NB - 1)], 7).wait_recv()
    update = jnp.concatenate(
        [update_buf[pl.ds(k, NB, stride=na), :] for k in range(na)], axis=0
    )
    pair_v[...] = (couple_v[...].astype(F32) + update).astype(BF16)
    pair_copy = pltpu.make_async_copy(pair_v, pair_out.at[0], out_sems.at[1])
    pair_copy.start()

    batch(small_buf.at[pl.ds(0, NB - 1)], 0).wait_send()
    batch(bias_buf.at[pl.ds(0, na - 1)], 1).wait_send()
    batch(x_buf.at[pl.ds(0, NB - 1)], 2).wait_send()
    batch(live_buf.at[pl.ds(0, na - 1)], 3).wait_send()
    batch(rows_buf.at[pl.ds(0, na - 1)], 4).wait_send()
    batch(left_buf.at[pl.ds(0, NB - 1)], 5).wait_send()
    batch(right_buf.at[pl.ds(0, na - 1)], 6).wait_send()
    batch(update_send.at[pl.ds(0, NB - 1)], 7).wait_send()
    align_copy.wait()
    pair_copy.wait()


def per_device(
    lineup, flags, couple, offset, w_row, w_row_out, w_col, w_col_out, w_first, w_second, w_final
):
    n = lineup.shape[1]
    na = n // NB
    vmem = pltpu.VMEM
    dma = pltpu.SemaphoreType.DMA
    align, pair = pl.pallas_call(
        functools.partial(kernel, na),
        out_shape=(
            jax.ShapeDtypeStruct((n, WIDTH), BF16),
            jax.ShapeDtypeStruct((1, n, PAIR), BF16),
        ),
        in_specs=[pl.BlockSpec(memory_space=pltpu.HBM)] * 10,
        out_specs=[pl.BlockSpec(memory_space=pltpu.HBM)] * 2,
        scratch_shapes=[
            vmem((n, WIDTH), BF16),
            vmem((1, n), jnp.int32),
            vmem((n, PAIR), BF16),
            vmem((HEADS, PAIR), BF16),
            vmem((WIDTH, 4 * WIDTH), BF16),
            vmem((WIDTH, WIDTH), BF16),
            vmem((WIDTH, 4 * WIDTH), BF16),
            vmem((WIDTH, WIDTH), BF16),
            vmem((2 * OUTER, WIDTH), BF16),
            vmem((OUTER * OUTER, PAIR), BF16),
            vmem((2, n, LANES), F32),
            vmem((na, 16, n), BF16),
            vmem((na * 16, n), F32),
            vmem((NB, na, 2 * WIDTH + n), BF16),
            vmem((NB, na, 2 * WIDTH + n), BF16),
            vmem((2 * NB, n), BF16),
            vmem((na, 2 * NB, n), BF16),
            vmem((NB, n, WIDTH), BF16),
            vmem((NB, na, WIDTH), BF16),
            vmem((2, n, LANES), F32),
            vmem((na, 2 * NB, LANES), BF16),
            vmem((na, 2 * NB, LANES), BF16),
            vmem((NB, OUTER, n), BF16),
            vmem((na, OUTER, n), BF16),
            vmem((OUTER * OUTER, LANES), F32),
            vmem((OUTER * LANES, PAIR), BF16),
            vmem((NB, na, PAIR), F32),
            vmem((n, PAIR), F32),
            vmem((n, WIDTH), BF16),
            vmem((n, PAIR), BF16),
            dma((10,)),
            dma((2,)),
            dma((8,)),
            dma((8,)),
            dma((NB,)),
        ],
        compiler_params=pltpu.CompilerParams(
            collective_id=0, has_side_effects=True, vmem_limit_bytes=32 * 1024 * 1024
        ),
    )(
        lineup,
        flags,
        couple,
        offset.T,
        w_row,
        w_row_out,
        w_col,
        w_col_out,
        jnp.concatenate([w_first.T, w_second.T], axis=0),
        w_final,
    )
    return align.reshape(n, 1, WIDTH), pair


def solution(mesh):
    return jax.shard_map(
        per_device,
        mesh=mesh,
        in_specs=(
            P(("dp", "dap"), None, None),
            P(("dp", "dap"), None),
            P(("dp", "dap"), None, None),
            P(),
            P(),
            P(),
            P(),
            P(),
            P(),
            P(),
            P(),
        ),
        out_specs=(P("dp", "dap", None), P(("dp", "dap"), None, None)),
        check_vma=False,
    )
```

time: 516 us -> 58.5 us (0.11)
  blocking collectives: 439 us -> 0 us
  Pallas kernels: 0 us -> 49.8 us
  starting transfers between devices: 26.5 us -> 0 us
  between operations: 14.5 us -> 0.67 us
  waiting for transfers between devices: 13.4 us -> 0 us
  other arithmetic: 7.88 us -> 0.77 us
    all_gather x2 -> x0, blocking collectives: 439 us -> none  [the longest x1 225 us: per_device(): full_bias = lax.all_gather(local_bias, 'dap', axis=1, tiled=True)]
    pallas_call x0 -> x1, Pallas kernels: none -> 49.8 us  [per_device(): pl.pallas_call(functools.partial(kernel, na), out_shape=(jax.ShapeDtypeSt...]
    all_to_all x2 -> x0, starting transfers between devices: 26.5 us -> none  [the longest x1 20.8 us: per_device(): lax.all_to_all(present_mask.astype(jnp.bfloat16), 'dap', split_axis=1, co...]
    all_to_all x2 -> x0, waiting for transfers between devices: 13.3 us -> none  [the longest x1 13.3 us: per_device(): lax.all_to_all(lineup_chain_slices, 'dap', split_axis=1, concat_axis=0, t...]
  transfers between devices with their start and end apart: 3 -> 0, of which waited for: 1 -> 0; matrix products, arithmetic and copies ran while one was open for 2% -> 0% of each run, Pallas kernels for 0% -> 0%
where the time goes in v1:
time: 58.5 us; the launch traced here: 58.1 us
  Pallas kernels  49.8 us (85%)
  local copies, waits for them, and re-layouts  6.89 us (12%)
  other arithmetic  0.77 us (1%)
  between operations  0.67 us (1%)
    pallas_call x1, Pallas kernels, per_device(): pl.pallas_call(functools.partial(kernel, na), out_shape=(jax.ShapeDtypeSt...  49.8 us
    unnamed x20, local copies, waits for them, and re-layouts  6.89 us

profile of v1, /device:TPU:1, one launch (start us, length us, event | category | flops | bytes accessed | tf_op | source)
XLA Modules:
  0.0 58.1 jit_solution(4149645037329569345)
XLA Ops:
  0.6 0.0 copy-start.5
  0.6 0.0 copy-start.7
  0.7 0.0 copy-start.8
  0.7 0.8 %pad_maximum_fusion.w_outer_t = bf16[64,256]{1,0:T(8,128)(2,1)S(1)} fusion(bf16[32,256]{1,0:T(8,128)(2,1)} %bitcast.6, bf16[32,256]{1,0:T(8,128)(2,1)} %bitcast.7), kind=kLoop, calls=%fused_computation | loop fusion | flops 65536 | bytes 65536 | tf_op jit(solution)/shard_map/concatenate | solution.py:450
  1.4 0.0 copy-done.5
  1.5 0.0 copy-done.7
  1.5 0.0 copy-done.8
  1.5 0.0 copy-start
  1.5 1.0 %copy-done = bf16[256,1024]{1,0:T(8,128)(2,1)S(1)} copy-done((bf16[256,1024]{1,0:T(8,128)(2,1)S(1)}, bf16[256,1024]{1,0:T(8,128)(2,1)}, u32[]{:S(2)}) %copy-start) | copy-done | bytes 524312
  2.5 0.0 copy-start.1
  2.5 1.0 %copy-done.1 = bf16[256,1024]{1,0:T(8,128)(2,1)S(1)} copy-done((bf16[256,1024]{1,0:T(8,128)(2,1)S(1)}, bf16[256,1024]{1,0:T(8,128)(2,1)}, u32[]{:S(2)}) %copy-start.1) | copy-done | bytes 524312
  3.6 0.0 copy-start.2
  3.6 0.9 %copy-done.2 = bf16[1024,128]{1,0:T(8,128)(2,1)S(1)} copy-done((bf16[1024,128]{1,0:T(8,128)(2,1)S(1)}, bf16[1024,128]{1,0:T(8,128)(2,1)}, u32[]{:S(2)}) %copy-start.2) | copy-done | bytes 262168
  4.5 0.0 copy-start.3
  4.5 0.9 %copy-done.3 = bf16[256,256]{1,0:T(8,128)(2,1)S(1)} copy-done((bf16[256,256]{1,0:T(8,128)(2,1)S(1)}, bf16[256,256]{1,0:T(8,128)(2,1)}, u32[]{:S(2)}) %copy-start.3) | copy-done | bytes 131096
  5.4 0.0 copy-start.4
  5.4 0.9 %copy-done.4 = bf16[256,256]{1,0:T(8,128)(2,1)S(1)} copy-done((bf16[256,256]{1,0:T(8,128)(2,1)S(1)}, bf16[256,256]{1,0:T(8,128)(2,1)}, u32[]{:S(2)}) %copy-start.4) | copy-done | bytes 131096
  6.3 0.0 copy-start.6
  6.3 0.8 %copy-done.6 = bf16[1,128,128]{2,1,0:T(8,128)(2,1)S(1)} copy-done((bf16[1,128,128]{2,1,0:T(8,128)(2,1)S(1)}, bf16[1,128,128]{2,1,0:T(8,128)(2,1)}, u32[]{:S(2)}) %copy-start.6) | copy-done | bytes 32792
  7.1 49.8 %shard_map.122 = (bf16[128,256]{1,0:T(8,128)(2,1)S(1)}, bf16[1,128,128]{2,1,0:T(8,128)(2,1)S(1)}) custom-call(bf16[1,128,256]{2,1,0:T(8,128)(2,1)S(1)} %copy-done.5, s32[1,128]{1,0:T(1,128)S(1)} %copy-done.8, bf16[1,128,128]{2,1,0:T(8,128)(2,1)S(1)} %copy-done.6, bf16[8,128]{1,0:T(8,128)(2,1)S(1)} %bitcast.5, bf16[256,1024]{1,0:T(8,128)(2,1)S(1)} %copy-done, ...), custom_call_target="tpu_custom_call" | custom-call | tf_op jit(solution)/shard_map/pallas_call | solution.py:393
  56.9 0.6 %copy.15 = bf16[128,1,256]{2,0,1:T(8,128)(2,1)} copy(bf16[128,1,256]{2,0,1:T(8,128)(2,1)S(1)} %bitcast.4) | data formatting | bytes 131072
  57.5 0.6 %copy.16 = bf16[1,128,128]{2,1,0:T(8,128)(2,1)} copy(bf16[1,128,128]{2,1,0:T(8,128)(2,1)S(1)} %get-tuple-element.9) | data formatting | bytes 65536
Async XLA Ops:
  0.6 0.8 %copy-start.5 = (bf16[1,128,256]{2,1,0:T(8,128)(2,1)S(1)}, bf16[1,128,256]{2,1,0:T(8,128)(2,1)}, u32[]{:S(2)}) copy-start(bf16[1,128,256]{2,1,0:T(8,128)(2,1)} %lineup.1) | copy-start | bytes 196612
  0.6 0.8 %copy-start.7 = (bf16[128,8]{0,1:T(8,128)(2,1)S(1)}, bf16[128,8]{0,1:T(8,128)(2,1)}, u32[]{:S(2)}) copy-start(bf16[128,8]{0,1:T(8,128)(2,1)} %param.14) | copy-start | bytes 6148
  0.7 0.8 %copy-start.8 = (s32[1,128]{1,0:T(1,128)S(1)}, s32[1,128]{1,0:T(1,128)}, u32[]{:S(2)}) copy-start(s32[1,128]{1,0:T(1,128)} %flags.1) | copy-start | bytes 1540
  1.5 1.0 %copy-start = (bf16[256,1024]{1,0:T(8,128)(2,1)S(1)}, bf16[256,1024]{1,0:T(8,128)(2,1)}, u32[]{:S(2)}) copy-start(bf16[256,1024]{1,0:T(8,128)(2,1)} %w_row.1) | copy-start | bytes 1572868
  2.5 1.0 %copy-start.1 = (bf16[256,1024]{1,0:T(8,128)(2,1)S(1)}, bf16[256,1024]{1,0:T(8,128)(2,1)}, u32[]{:S(2)}) copy-start(bf16[256,1024]{1,0:T(8,128)(2,1)} %w_col.1) | copy-start | bytes 1572868
  3.6 0.9 %copy-start.2 = (bf16[1024,128]{1,0:T(8,128)(2,1)S(1)}, bf16[1024,128]{1,0:T(8,128)(2,1)}, u32[]{:S(2)}) copy-start(bf16[1024,128]{1,0:T(8,128)(2,1)} %w_final.1) | copy-start | bytes 786436
  4.5 0.9 %copy-start.3 = (bf16[256,256]{1,0:T(8,128)(2,1)S(1)}, bf16[256,256]{1,0:T(8,128)(2,1)}, u32[]{:S(2)}) copy-start(bf16[256,256]{1,0:T(8,128)(2,1)} %w_row_out.1) | copy-start | bytes 393220
  5.4 0.9 %copy-start.4 = (bf16[256,256]{1,0:T(8,128)(2,1)S(1)}, bf16[256,256]{1,0:T(8,128)(2,1)}, u32[]{:S(2)}) copy-start(bf16[256,256]{1,0:T(8,128)(2,1)} %w_col_out.1) | copy-start | bytes 393220
  6.3 0.8 %copy-start.6 = (bf16[1,128,128]{2,1,0:T(8,128)(2,1)S(1)}, bf16[1,128,128]{2,1,0:T(8,128)(2,1)}, u32[]{:S(2)}) copy-start(bf16[1,128,128]{2,1,0:T(8,128)(2,1)} %couple.1) | copy-start | bytes 98308

commit v2 on v1

--- a/solution.py
+++ b/solution.py
@@ -15,7 +15,9 @@
 LANES = 128
 EPS = 1e-5
 MASKED = 1e9
-NB = 8
+NZ, NX, NC = 2, 4, 2
+NB = NX * NC
+NF = NZ * NX
 
 F32 = jnp.float32
 BF16 = jnp.bfloat16
@@ -56,7 +58,8 @@
     w_row_out,
     w_col,
     w_col_out,
-    w_outer_t,
+    w_first_t,
+    w_second_t,
     w_final,
     align_out,
     pair_out,
@@ -88,33 +91,51 @@
     final_rep,
     update_send,
     update_buf,
-    align_v,
-    pair_v,
+    gates_v,
+    values_v,
+    scores_v,
     in_sems,
-    out_sems,
     send_sems,
     recv_sems,
     x_sems,
 ):
     n = na * NB
+    ny = na // NZ
+    ne = ny * NC
     me = lax.axis_index("dap")
     a, b = me // NB, me % NB
+    y, z, x_at, c = a // NZ, a % NZ, b // NC, b % NC
+    e, f = c * ny + y, z * NX + x_at
+
+    def around(size, r):
+        return min(r, size - r)
 
     def b_mate(r):
-        return (b + r) % NB
+        return (x_at + r // NC) % NX * NC + (c + r) % NC
 
     def a_mate(r):
-        return (a + r) % na
+        return (y + r // NZ) % ny * NZ + (z + r) % NZ
+
+    def e_mate(r):
+        return (c + r // ny) % NC * ny + (y + r) % ny
+
+    def f_mate(r):
+        return (z + r // NX) % NZ * NX + (x_at + r) % NX
+
+    def from_ef(e_at, f_at):
+        return ((e_at % ny * NZ + f_at // NX) * NX + f_at % NX) * NC + e_at // ny
+
+    b_far = sorted(range(1, NB), key=lambda r: -around(NX, r // NC) * 2 - r % NC)
+    a_far = sorted(range(1, na), key=lambda r: -around(ny, r // NZ) - 4 * (r % NZ))
+    e_far = sorted(range(1, ne), key=lambda r: -around(ny, r % ny) * 2 - r // ny)
+    f_far = sorted(range(1, NF), key=lambda r: -around(NX, r % NX) - 4 * (r // NX))
+    y_far = [r for r in a_far if r % NZ == 0]
+
+    back = {r: (NX - r // NC) % NX * NC + r % NC for r in range(1, NB)}
 
     barrier = pltpu.get_barrier_semaphore()
-    for r in range(1, NB):
-        pl.semaphore_signal(
-            barrier, inc=1, device_id={"dap": a * NB + b_mate(r)}, device_id_type=MESH
-        )
-    for r in range(1, na):
-        pl.semaphore_signal(
-            barrier, inc=1, device_id={"dap": a_mate(r) * NB + b}, device_id_type=MESH
-        )
+    for mate in [a_mate(r) * NB + b for r in [1] + y_far] + [a * NB + b_mate(r) for r in b_far]:
+        pl.semaphore_signal(barrier, inc=1, device_id={"dap": mate}, device_id_type=MESH)
 
     pairs = (
         (lineup.at[0], lineup_v),
@@ -125,7 +146,8 @@
         (w_row_out, w_row_out_v),
         (w_col, w_col_v),
         (w_col_out, w_col_out_v),
-        (w_outer_t, w_outer_v),
+        (w_first_t, w_outer_v.at[:OUTER]),
+        (w_second_t, w_outer_v.at[OUTER:]),
         (w_final, w_final_v),
     )
     loads = [pltpu.make_async_copy(src, dst, in_sems.at[k]) for k, (src, dst) in enumerate(pairs)]
@@ -186,14 +208,13 @@
     bias = dot_nt(offset_v[...], normed(pair))
     bias_buf[a] = jnp.concatenate([bias, jnp.zeros_like(bias)], axis=0).astype(BF16)
 
-    pl.semaphore_wait(barrier, NB + na - 2)
-
-    for r in range(1, NB):
+    pl.semaphore_wait(barrier, NB + ny - 1)
+
+    send(bias_buf.at[a], bias_buf.at[a], 8, a_mate(1) * NB + b)
+    for r in b_far:
         mate = b_mate(r)
         send(small_send.at[mate], small_buf.at[b], 0, a * NB + mate)
-    for r in range(1, na):
-        send(bias_buf.at[a], bias_buf.at[a], 1, a_mate(r) * NB + b)
-    for r in range(1, NB):
+    for r in b_far:
         pltpu.make_async_remote_copy(
             src_ref=x_buf.at[b],
             dst_ref=x_buf.at[b],
@@ -204,58 +225,62 @@
         ).start()
     small_buf[b] = small_send[b]
 
-    loads[9].wait()
-    products[...] = w_final_v[...].astype(F32)
-    for d in range(OUTER):
-        part = products[pl.ds(d, OUTER, stride=OUTER), :].astype(BF16)
-        for k in range(4):
-            final_rep[pl.ds((d * 4 + k) * OUTER, OUTER), :] = part
+    loads[10].wait()
+    for k in range(OUTER):
+        part = w_final_v[k * OUTER : (k + 1) * OUTER, :]
+        for copy in range(4):
+            at = (k * 4 + copy) * OUTER
+            final_rep[at : at + OUTER, :] = part
 
     batch(small_buf.at[pl.ds(0, NB - 1)], 0).wait_recv()
-    small = small_buf[...]
-    live8 = small[:, :8, 2 * WIDTH :].astype(F32)[:, 0, :]
-    live_send[...] = jnp.concatenate([live8, live8], axis=0).astype(BF16)
-    for r in range(1, na):
-        send(live_send, live_buf.at[a], 3, a_mate(r) * NB + b)
-    live_buf[a] = live_send[...]
+    batch(bias_buf.at[0], 8).wait_recv()
+    two = bias_buf.at[pl.ds(y * NZ, NZ)]
+    for r in y_far:
+        send(two, two, 1, a_mate(r) * NB + b)
 
     loads[4].wait()
-    queries_in = small[:, :, WIDTH : 2 * WIDTH].reshape(NB * na, WIDTH)
+    queries_in = small_buf[:, :, WIDTH : 2 * WIDTH].reshape(NB * na, WIDTH)
     queries = (dot(queries_in, w_row_v[:, :WIDTH]) * HEAD_DIM**-0.5).astype(BF16)
-    gates = jax.nn.sigmoid(dot(queries_in, w_row_v[:, 3 * WIDTH :]))
-    rows_wide[0] = gates[:, :LANES]
-    rows_wide[1] = gates[:, LANES:]
+    gates_v[...] = jax.nn.sigmoid(dot(queries_in, w_row_v[:, 3 * WIDTH :])).reshape(
+        NB, na, WIDTH
+    )
     gated_buf[...] = queries.reshape(NB, na, WIDTH)
 
-    batch(bias_buf.at[pl.ds(0, na - 1)], 1).wait_recv()
-    bias_wide[...] = bias_buf[...].astype(F32).reshape(na * 16, n)
-    score_bias = jnp.concatenate(
-        [bias_wide[pl.ds(h, na, stride=16), :] for h in range(HEADS)], axis=0
-    )
     own_head = head_mask(na)
-    lane_head = iota((na, WIDTH), 1) // HEAD_DIM
-    ones = jnp.ones((n, LANES), BF16)
-
-    for r in range(NB):
-        seq = (b + NB - r) % NB
+    for r in [0] + b_far[::-1]:
+        seq = b_mate(r)
         if r > 0:
             pltpu.make_async_remote_copy(
                 src_ref=x_buf.at[seq],
                 dst_ref=x_buf.at[seq],
                 send_sem=send_sems.at[2],
-                recv_sem=x_sems.at[r],
+                recv_sem=x_sems.at[back[r]],
                 device_id={"dap": a * NB + b_mate(1)},
                 device_id_type=MESH,
             ).wait_recv()
         kv = dot(x_buf[seq], w_row_v[:, WIDTH : 3 * WIDTH]).astype(BF16)
-        keys, values = kv[:, :WIDTH], kv[:, WIDTH:]
-        query = gated_buf[seq]
-        spread = jnp.where(own_head, jnp.concatenate([query] * HEADS, axis=0), 0)
-        scores = dot_nt(spread, keys)
+        values_v[seq] = kv[:, WIDTH:]
+        spread = jnp.where(own_head, jnp.concatenate([gated_buf[seq]] * HEADS, axis=0), 0)
         key_live = small_buf[seq, :, 2 * WIDTH :].astype(F32)[:1]
-        scores = scores + (key_live - 1.0) * MASKED + score_bias
+        scores_v[seq] = dot_nt(spread, kv[:, :WIDTH]) + (key_live - 1.0) * MASKED
+
+    batch(bias_buf.at[pl.ds(0, na - NZ)], 1).wait_recv()
+    live8 = small_buf[:, :8, 2 * WIDTH :].astype(F32)[:, 0, :]
+    live_send[...] = jnp.concatenate([live8, live8], axis=0).astype(BF16)
+    for r in a_far:
+        send(live_send, live_buf.at[a], 3, a_mate(r) * NB + b)
+    live_buf[a] = live_send[...]
+
+    bias_wide[...] = bias_buf[...].astype(F32).reshape(na * 16, n)
+    score_bias = jnp.concatenate(
+        [bias_wide[pl.ds(h, na, stride=16), :] for h in range(HEADS)], axis=0
+    )
+    lane_head = iota((na, WIDTH), 1) // HEAD_DIM
+    ones = jnp.ones((n, LANES), BF16)
+    for seq in range(NB):
+        scores = scores_v[seq] + score_bias
         expo = jnp.exp(scores - jnp.max(scores, axis=-1, keepdims=True)).astype(BF16)
-        mixed = dot(expo, values)
+        mixed = dot(expo, values_v[seq])
         total = dot(expo, ones)
         top, bottom = mixed[:na], jnp.concatenate([total[:na]] * 2, axis=1)
         for h in range(1, HEADS):
@@ -264,9 +289,7 @@
             bottom = jnp.where(
                 lane_head == h, jnp.concatenate([total[rows]] * 2, axis=1), bottom
             )
-        at = pl.ds(pl.multiple_of(seq * na, na), na)
-        gate = jnp.concatenate([rows_wide[0, at, :], rows_wide[1, at, :]], axis=1)
-        gated_buf[seq] = (gate * (top / bottom)).astype(BF16)
+        gated_buf[seq] = (gates_v[seq] * (top / bottom)).astype(BF16)
 
     loads[5].wait()
     grown = dot(gated_buf[...].reshape(NB * na, WIDTH), w_row_out_v[...])
@@ -277,7 +300,7 @@
         rows_send[k] = jnp.concatenate(
             [rows_wide[h, pl.ds(k, NB, stride=na), :] for h in range(2)], axis=0
         ).astype(BF16)
-    for r in range(1, na):
+    for r in a_far:
         mate = a_mate(r)
         send(rows_send.at[mate], rows_buf.at[a], 4, mate * NB + b)
     rows_buf[a] = rows_send[a]
@@ -287,8 +310,13 @@
     own = (iota((16, n), 1) == b * na + a).astype(BF16)
     own_live = dot_nt(own, live_all)[:1]
     pick = (NB * na, n)
-    pick_i = (iota(pick, 1) == (iota(pick, 0) // na) * na + a).astype(BF16)
-    pick_j = (iota(pick, 1) == iota(pick, 0) % na + b * na).astype(BF16)
+    tile_e, tile_f = iota(pick, 0) % ne, iota(pick, 0) // ne
+
+    def place(y_at, z_at, x_of, core):
+        return (x_of * NC + core) * na + y_at * NZ + z_at
+
+    pick_i = (iota(pick, 1) == place(tile_e % ny, z, x_at, tile_e // ny)).astype(BF16)
+    pick_j = (iota(pick, 1) == place(y, tile_f // NX, tile_f % NX, c)).astype(BF16)
     counts = jnp.sum(
         dot_nt(pick_i, live_all) * dot_nt(pick_j, live_all), axis=-1, keepdims=True
     )
@@ -300,6 +328,7 @@
     loads[6].wait()
     loads[7].wait()
     loads[8].wait()
+    loads[9].wait()
 
     batch(rows_buf.at[pl.ds(0, na - 1)], 4).wait_recv()
     arrived = rows_buf[...].astype(F32)
@@ -320,37 +349,35 @@
     mixed = dot(expo, jnp.concatenate(spread_values, axis=0)) / dot(expo, ones_bd)
     gated = (jax.nn.sigmoid(mapped[:, 3 * WIDTH :]) * mixed).astype(BF16)
     updated = (column + dot(gated, w_col_out_v[...])).astype(BF16)
-    align_v[...] = updated
-    align_copy = pltpu.make_async_copy(align_v, align_out, out_sems.at[0])
-    align_copy.start()
+    align_out[...] = updated
 
     outer = (dot_nt(w_outer_v[...], normed(updated.astype(F32))) * own_live).astype(BF16)
-    left_buf[b] = outer[:OUTER]
-    right_buf[a] = outer[OUTER:]
-    for r in range(1, na):
-        send(right_buf.at[a], right_buf.at[a], 6, a_mate(r) * NB + b)
-    for r in range(1, NB):
-        send(left_buf.at[b], left_buf.at[b], 5, a * NB + b_mate(r))
-    batch(left_buf.at[pl.ds(0, NB - 1)], 5).wait_recv()
-    batch(right_buf.at[pl.ds(0, na - 1)], 6).wait_recv()
-    lefts = left_buf[...].reshape(NB * OUTER, n)
-    rights = right_buf[...].reshape(na * OUTER, n)
-    product = dot_nt(rights, lefts)
-    depth = na * OUTER
+    left_buf[e] = outer[:OUTER]
+    right_buf[f] = outer[OUTER:]
+    for r in f_far:
+        send(right_buf.at[f], right_buf.at[f], 6, from_ef(e, f_mate(r)))
+    for r in e_far:
+        send(left_buf.at[e], left_buf.at[e], 5, from_ef(e_mate(r), f))
+    batch(left_buf.at[pl.ds(0, ne - 1)], 5).wait_recv()
+    batch(right_buf.at[pl.ds(0, NF - 1)], 6).wait_recv()
+    lefts = left_buf[...].reshape(ne * OUTER, n)
+    rights = right_buf[...].reshape(NF * OUTER, n)
+    product = dot_nt(lefts, rights)
+    depth = ne * OUTER
     products[pl.ds(0, depth), :] = product[:, :LANES]
     products[pl.ds(depth, depth), :] = product[:, LANES:]
-    quarter = iota((na, LANES), 1) // OUTER
+    quarter = iota((ne, LANES), 1) // OUTER
     step = 8
     total = None
     for first in range(0, OUTER, step):
         slabs = []
-        for d in range(first, first + step):
+        for k in range(first, first + step):
             tiles = [
-                products[pl.ds(t * depth + d, na, stride=OUTER), :].astype(BF16) for t in range(2)
+                products[pl.ds(t * depth + k, ne, stride=OUTER), :].astype(BF16) for t in range(2)
             ]
             slabs.append(
                 jnp.concatenate(
-                    [jnp.where(quarter == i % 4, tiles[i // 4], 0) for i in range(NB)], axis=0
+                    [jnp.where(quarter == j % 4, tiles[j // 4], 0) for j in range(NF)], axis=0
                 )
             )
         term = dot(
@@ -358,29 +385,29 @@
             final_rep[pl.ds(first * LANES, step * LANES), :],
         )
         total = term if total is None else total + term
-    update_send[...] = (total / counts).reshape(NB, na, PAIR)
-    for r in range(1, NB):
-        mate = b_mate(r)
-        send(update_send.at[mate], update_buf.at[pl.ds(b * na, na)], 7, a * NB + mate)
-    update_buf[pl.ds(b * na, na)] = update_send[b]
-    batch(update_send.at[pl.ds(0, NB - 1)], 7).wait_recv()
-    update = jnp.concatenate(
-        [update_buf[pl.ds(k, NB, stride=na), :] for k in range(na)], axis=0
-    )
-    pair_v[...] = (couple_v[...].astype(F32) + update).astype(BF16)
-    pair_copy = pltpu.make_async_copy(pair_v, pair_out.at[0], out_sems.at[1])
-    pair_copy.start()
+    rows_wide[0] = total / counts
+    for k in range(ne):
+        update_send[k] = rows_wide[0, pl.ds(k, NF, stride=ne), :]
+    for r in e_far:
+        mate = e_mate(r)
+        send(update_send.at[mate], update_buf.at[e], 7, from_ef(mate, f))
+    update_buf[e] = update_send[e]
+    wide[1] = couple_v[...].astype(F32)
+    batch(update_send.at[pl.ds(0, ne - 1)], 7).wait_recv()
+    for k in range(ne):
+        at = pl.ds(k % ny * (NF * NC) + k // ny, NF, stride=NC)
+        wide[1, at, :] = wide[1, at, :] + update_buf[k]
+    pair_out[0] = wide[1].astype(BF16)
 
     batch(small_buf.at[pl.ds(0, NB - 1)], 0).wait_send()
-    batch(bias_buf.at[pl.ds(0, na - 1)], 1).wait_send()
+    batch(bias_buf.at[0], 8).wait_send()
+    batch(bias_buf.at[pl.ds(0, na - NZ)], 1).wait_send()
     batch(x_buf.at[pl.ds(0, NB - 1)], 2).wait_send()
     batch(live_buf.at[pl.ds(0, na - 1)], 3).wait_send()
     batch(rows_buf.at[pl.ds(0, na - 1)], 4).wait_send()
-    batch(left_buf.at[pl.ds(0, NB - 1)], 5).wait_send()
-    batch(right_buf.at[pl.ds(0, na - 1)], 6).wait_send()
-    batch(update_send.at[pl.ds(0, NB - 1)], 7).wait_send()
-    align_copy.wait()
-    pair_copy.wait()
+    batch(left_buf.at[pl.ds(0, ne - 1)], 5).wait_send()
+    batch(right_buf.at[pl.ds(0, NF - 1)], 6).wait_send()
+    batch(update_send.at[pl.ds(0, ne - 1)], 7).wait_send()
 
 
 def per_device(
@@ -388,16 +415,17 @@
 ):
     n = lineup.shape[1]
     na = n // NB
+    ne = na // NZ * NC
     vmem = pltpu.VMEM
     dma = pltpu.SemaphoreType.DMA
     align, pair = pl.pallas_call(
         functools.partial(kernel, na),
         out_shape=(
-            jax.ShapeDtypeStruct((n, WIDTH), BF16),
-            jax.ShapeDtypeStruct((1, n, PAIR), BF16),
+            vmem((n, WIDTH), BF16),
+            vmem((1, n, PAIR), BF16),
         ),
-        in_specs=[pl.BlockSpec(memory_space=pltpu.HBM)] * 10,
-        out_specs=[pl.BlockSpec(memory_space=pltpu.HBM)] * 2,
+        in_specs=[pl.BlockSpec(memory_space=pltpu.HBM)] * 11,
+        out_specs=[pl.BlockSpec(memory_space=vmem)] * 2,
         scratch_shapes=[
             vmem((n, WIDTH), BF16),
             vmem((1, n), jnp.int32),
@@ -421,34 +449,40 @@
             vmem((2, n, LANES), F32),
             vmem((na, 2 * NB, LANES), BF16),
             vmem((na, 2 * NB, LANES), BF16),
-            vmem((NB, OUTER, n), BF16),
-            vmem((na, OUTER, n), BF16),
+            vmem((ne, OUTER, n), BF16),
+            vmem((NF, OUTER, n), BF16),
             vmem((OUTER * OUTER, LANES), F32),
             vmem((OUTER * LANES, PAIR), BF16),
-            vmem((NB, na, PAIR), F32),
-            vmem((n, PAIR), F32),
-            vmem((n, WIDTH), BF16),
-            vmem((n, PAIR), BF16),
-            dma((10,)),
-            dma((2,)),
-            dma((8,)),
-            dma((8,)),
+            vmem((ne, NF, PAIR), F32),
+            vmem((ne, NF, PAIR), F32),
+            vmem((NB, na, WIDTH), F32),
+            vmem((NB, n, WIDTH), BF16),
+            vmem((NB, HEADS * na, n), F32),
+            dma((11,)),
+            dma((9,)),
+            dma((9,)),
             dma((NB,)),
         ],
         compiler_params=pltpu.CompilerParams(
             collective_id=0, has_side_effects=True, vmem_limit_bytes=32 * 1024 * 1024
         ),
     )(
-        lineup,
-        flags,
-        couple,
-        offset.T,
-        w_row,
-        w_row_out,
-        w_col,
-        w_col_out,
-        jnp.concatenate([w_first.T, w_second.T], axis=0),
-        w_final,
+        *[
+            pltpu.with_memory_space_constraint(v, pltpu.HBM)
+            for v in (
+                lineup,
+                flags,
+                couple,
+                offset.T,
+                w_row,
+                w_row_out,
+                w_col,
+                w_col_out,
+                w_first.T,
+                w_second.T,
+                w_final,
+            )
+        ]
     )
     return align.reshape(n, 1, WIDTH), pair
 

time: 58.5 us -> 47.5 us (0.81)
  local copies, waits for them, and re-layouts: 6.89 us -> 1.25 us
  Pallas kernels: 49.8 us -> 45.5 us
  other arithmetic: 0.77 us -> 0 us
    unnamed x20 -> x2, local copies, waits for them, and re-layouts: 6.89 us -> 1.25 us
    pallas_call x1, Pallas kernels: 49.8 us -> 45.5 us  [per_device(): pl.pallas_call(functools.partial(kernel, na), out_shape=(vmem((n, WIDTH),...]
    concatenate x1 -> x0, other arithmetic: 0.77 us -> none  [per_device(): jnp.concatenate([w_first.T, w_second.T], axis=0)]
where the time goes in v2:
time: 47.5 us; the launch traced here: 47.4 us
  Pallas kernels  45.5 us (96%)
  local copies, waits for them, and re-layouts  1.25 us (3%)
  between operations  0.64 us (1%)
    pallas_call x1, Pallas kernels, per_device(): pl.pallas_call(functools.partial(kernel, na), out_shape=(vmem((n, WIDTH),...  45.5 us
    unnamed x2, local copies, waits for them, and re-layouts  1.25 us

profile of v2, /device:TPU:1, one launch (start us, length us, event | category | flops | bytes accessed | tf_op | source)
XLA Modules:
  0.0 47.4 jit_solution(11953664826697173159)
XLA Ops:
  0.6 45.5 %shard_map.122 = (bf16[128,256]{1,0:T(8,128)(2,1)S(1)}, bf16[1,128,128]{2,1,0:T(8,128)(2,1)S(1)}) custom-call(bf16[1,128,256]{2,1,0:T(8,128)(2,1)} %lineup.1, s32[1,128]{1,0:T(1,128)} %flags.1, bf16[1,128,128]{2,1,0:T(8,128)(2,1)} %couple.1, bf16[8,128]{1,0:T(8,128)(2,1)} %bitcast.7, bf16[256,1024]{1,0:T(8,128)(2,1)} %w_row.1, bf16[256,256]{1,0:T(8,128)(2,1)} %w_row_out.1, ...), custom_call_target="tpu_custom_call" | custom-call | tf_op jit(solution)/shard_map/pallas_call | solution.py:421
  46.1 0.6 %copy.15 = bf16[128,1,256]{2,0,1:T(8,128)(2,1)} copy(bf16[128,1,256]{2,0,1:T(8,128)(2,1)S(1)} %bitcast.4) | data formatting | bytes 131072
  46.8 0.6 %copy.16 = bf16[1,128,128]{2,1,0:T(8,128)(2,1)} copy(bf16[1,128,128]{2,1,0:T(8,128)(2,1)S(1)} %get-tuple-element.7) | data formatting | bytes 65536

commit v3 on v2

--- a/solution.py
+++ b/solution.py
@@ -63,8 +63,6 @@
     w_final,
     align_out,
     pair_out,
-    lineup_v,
-    flags_v,
     couple_v,
     offset_v,
     w_row_v,
@@ -76,8 +74,8 @@
     wide,
     bias_buf,
     bias_wide,
-    small_send,
-    small_buf,
+    flag_buf,
+    raw_v,
     live_send,
     live_buf,
     x_buf,
@@ -131,15 +129,13 @@
     f_far = sorted(range(1, NF), key=lambda r: -around(NX, r % NX) - 4 * (r // NX))
     y_far = [r for r in a_far if r % NZ == 0]
 
-    back = {r: (NX - r // NC) % NX * NC + r % NC for r in range(1, NB)}
-
     barrier = pltpu.get_barrier_semaphore()
     for mate in [a_mate(r) * NB + b for r in [1] + y_far] + [a * NB + b_mate(r) for r in b_far]:
         pl.semaphore_signal(barrier, inc=1, device_id={"dap": mate}, device_id_type=MESH)
 
     pairs = (
-        (lineup.at[0], lineup_v),
-        (flags, flags_v),
+        (lineup.at[0], x_buf.at[b]),
+        (flags, flag_buf.at[b]),
         (couple.at[0], couple_v),
         (offset_t, offset_v),
         (w_row, w_row_v),
@@ -151,8 +147,8 @@
         (w_final, w_final_v),
     )
     loads = [pltpu.make_async_copy(src, dst, in_sems.at[k]) for k, (src, dst) in enumerate(pairs)]
-    for load in loads:
-        load.start()
+    for k in (2, 3, 0, 1, 4, 5, 6, 7, 8, 9, 10):
+        loads[k].start()
 
     def send(src, dst, phase, device):
         copy = pltpu.make_async_remote_copy(
@@ -175,55 +171,32 @@
             device_id_type=MESH,
         )
 
-    loads[0].wait()
-    x = lineup_v[...].astype(F32)
-    wide[0] = x[:, :LANES]
-    wide[1] = x[:, LANES:]
-    raw = jnp.concatenate(
-        [
-            jnp.concatenate([wide[h, pl.ds(k, na, stride=NB), :] for k in range(NB)], axis=0)
-            for h in range(2)
-        ],
-        axis=1,
-    )
-    x_norm = normed(raw)
-    x_buf[b] = x_norm
-
-    loads[1].wait()
-    order = (iota((n, n), 1) == (iota((n, n), 0) % na) * NB + iota((n, n), 0) // na).astype(BF16)
-    live = dot_nt(
-        jnp.broadcast_to(flags_v[...], (2 * NB, n)).astype(F32).astype(BF16), order
-    )
-    raw16 = raw.astype(BF16)
-    for k in range(NB):
-        rows = slice(k * na, (k + 1) * na)
-        small_send[k] = jnp.concatenate(
-            [raw16[rows], x_norm[rows], jnp.broadcast_to(live[:1], (na, n)).astype(BF16)], axis=1
+    def x_copy(src, slot, step, mate):
+        return pltpu.make_async_remote_copy(
+            src_ref=src,
+            dst_ref=x_buf.at[slot],
+            send_sem=send_sems.at[2],
+            recv_sem=x_sems.at[step],
+            device_id={"dap": a * NB + mate},
+            device_id_type=MESH,
         )
 
     loads[2].wait()
     loads[3].wait()
-    wide[0, :, :PAIR] = couple_v[...].astype(F32)
-    pair = jnp.concatenate([wide[0, pl.ds(k, na, stride=NB), :] for k in range(NB)], axis=0)
-    bias = dot_nt(offset_v[...], normed(pair))
+    bias = dot_nt(offset_v[...], normed(couple_v[...].astype(F32)))
     bias_buf[a] = jnp.concatenate([bias, jnp.zeros_like(bias)], axis=0).astype(BF16)
 
     pl.semaphore_wait(barrier, NB + ny - 1)
 
     send(bias_buf.at[a], bias_buf.at[a], 8, a_mate(1) * NB + b)
+    for r in y_far:
+        send(bias_buf.at[a], bias_buf.at[a], 1, a_mate(r) * NB + b)
     for r in b_far:
-        mate = b_mate(r)
-        send(small_send.at[mate], small_buf.at[b], 0, a * NB + mate)
-    for r in b_far:
-        pltpu.make_async_remote_copy(
-            src_ref=x_buf.at[b],
-            dst_ref=x_buf.at[b],
-            send_sem=send_sems.at[2],
-            recv_sem=x_sems.at[r],
-            device_id={"dap": a * NB + b_mate(r)},
-            device_id_type=MESH,
-        ).start()
-    small_buf[b] = small_send[b]
+        send(flags, flag_buf.at[b], 0, a * NB + b_mate(r))
+    along_x = sorted(range(1, NX), key=lambda d: around(NX, d))
+    for d in along_x:
+        x_copy(lineup.at[0], b, (NX - d) % NX * NC, b_mate(d * NC)).start()
+    x_copy(lineup.at[0], b, 1, b_mate(1)).start()
 
     loads[10].wait()
     for k in range(OUTER):
@@ -232,40 +205,48 @@
             at = (k * 4 + copy) * OUTER
             final_rep[at : at + OUTER, :] = part
 
-    batch(small_buf.at[pl.ds(0, NB - 1)], 0).wait_recv()
+    loads[4].wait()
+    own_head = head_mask(na)
+    pick_query = (iota((na, n), 1) == iota((na, n), 0) * NB + b).astype(BF16)
+
+    def project(r):
+        seq = b_mate(r)
+        x = x_buf[seq]
+        x_norm = normed(x.astype(F32))
+        raw_v[seq] = dot(pick_query, x)
+        query_in = dot(pick_query, x_norm).astype(BF16)
+        query = (dot(query_in, w_row_v[:, :WIDTH]) * HEAD_DIM**-0.5).astype(BF16)
+        gates_v[seq] = jax.nn.sigmoid(dot(query_in, w_row_v[:, 3 * WIDTH :]))
+        kv = dot(x_norm, w_row_v[:, WIDTH : 3 * WIDTH]).astype(BF16)
+        values_v[seq] = kv[:, WIDTH:]
+        spread = jnp.where(own_head, jnp.concatenate([query] * HEADS, axis=0), 0)
+        key_live = flag_buf[seq].astype(F32)
+        scores_v[seq] = dot_nt(spread, kv[:, :WIDTH]) + (key_live - 1.0) * MASKED
+
+    batch(flag_buf.at[pl.ds(0, NB - 1)], 0).wait_recv()
+    loads[0].wait()
+    loads[1].wait()
+    project(0)
+    x_copy(lineup.at[0], b_mate(1), 1, b_mate(1)).wait_recv()
+    project(1)
     batch(bias_buf.at[0], 8).wait_recv()
-    two = bias_buf.at[pl.ds(y * NZ, NZ)]
+    partner = bias_buf.at[a_mate(1)]
     for r in y_far:
-        send(two, two, 1, a_mate(r) * NB + b)
-
-    loads[4].wait()
-    queries_in = small_buf[:, :, WIDTH : 2 * WIDTH].reshape(NB * na, WIDTH)
-    queries = (dot(queries_in, w_row_v[:, :WIDTH]) * HEAD_DIM**-0.5).astype(BF16)
-    gates_v[...] = jax.nn.sigmoid(dot(queries_in, w_row_v[:, 3 * WIDTH :])).reshape(
-        NB, na, WIDTH
-    )
-    gated_buf[...] = queries.reshape(NB, na, WIDTH)
-
-    own_head = head_mask(na)
-    for r in [0] + b_far[::-1]:
-        seq = b_mate(r)
-        if r > 0:
-            pltpu.make_async_remote_copy(
-                src_ref=x_buf.at[seq],
-                dst_ref=x_buf.at[seq],
-                send_sem=send_sems.at[2],
-                recv_sem=x_sems.at[back[r]],
-                device_id={"dap": a * NB + b_mate(1)},
-                device_id_type=MESH,
-            ).wait_recv()
-        kv = dot(x_buf[seq], w_row_v[:, WIDTH : 3 * WIDTH]).astype(BF16)
-        values_v[seq] = kv[:, WIDTH:]
-        spread = jnp.where(own_head, jnp.concatenate([gated_buf[seq]] * HEADS, axis=0), 0)
-        key_live = small_buf[seq, :, 2 * WIDTH :].astype(F32)[:1]
-        scores_v[seq] = dot_nt(spread, kv[:, :WIDTH]) + (key_live - 1.0) * MASKED
-
-    batch(bias_buf.at[pl.ds(0, na - NZ)], 1).wait_recv()
-    live8 = small_buf[:, :8, 2 * WIDTH :].astype(F32)[:, 0, :]
+        send(partner, partner, 9, a_mate(r) * NB + b)
+    for d in along_x:
+        slot = b_mate(d * NC)
+        x_copy(lineup.at[0], slot, d * NC, b_mate(1)).wait_recv()
+        x_copy(x_buf.at[slot], slot, d * NC + 1, b_mate(1)).start()
+    for d in along_x:
+        project(d * NC)
+    for d in along_x:
+        x_copy(lineup.at[0], b_mate(d * NC + 1), d * NC + 1, b_mate(1)).wait_recv()
+    for d in along_x:
+        project(d * NC + 1)
+
+    batch(bias_buf.at[pl.ds(0, ny - 1)], 1).wait_recv()
+    batch(bias_buf.at[pl.ds(0, ny - 1)], 9).wait_recv()
+    live8 = jnp.concatenate([flag_buf[k] for k in range(NB)], axis=0).astype(F32)
     live_send[...] = jnp.concatenate([live8, live8], axis=0).astype(BF16)
     for r in a_far:
         send(live_send, live_buf.at[a], 3, a_mate(r) * NB + b)
@@ -293,7 +274,7 @@
 
     loads[5].wait()
     grown = dot(gated_buf[...].reshape(NB * na, WIDTH), w_row_out_v[...])
-    grown = small_buf[:, :, :WIDTH].reshape(NB * na, WIDTH).astype(F32) + grown
+    grown = raw_v[...].reshape(NB * na, WIDTH) + grown
     rows_wide[0] = grown[:, :LANES]
     rows_wide[1] = grown[:, LANES:]
     for k in range(na):
@@ -307,13 +288,13 @@
 
     batch(live_buf.at[pl.ds(0, na - 1)], 3).wait_recv()
     live_all = live_buf[...].astype(F32)[:, :NB].reshape(n, n).astype(BF16)
-    own = (iota((16, n), 1) == b * na + a).astype(BF16)
+    own = (iota((16, n), 1) == me).astype(BF16)
     own_live = dot_nt(own, live_all)[:1]
     pick = (NB * na, n)
     tile_e, tile_f = iota(pick, 0) % ne, iota(pick, 0) // ne
 
     def place(y_at, z_at, x_of, core):
-        return (x_of * NC + core) * na + y_at * NZ + z_at
+        return ((y_at * NZ + z_at) * NX + x_of) * NC + core
 
     pick_i = (iota(pick, 1) == place(tile_e % ny, z, x_at, tile_e // ny)).astype(BF16)
     pick_j = (iota(pick, 1) == place(y, tile_f // NX, tile_f % NX, c)).astype(BF16)
@@ -399,9 +380,10 @@
         wide[1, at, :] = wide[1, at, :] + update_buf[k]
     pair_out[0] = wide[1].astype(BF16)
 
-    batch(small_buf.at[pl.ds(0, NB - 1)], 0).wait_send()
+    batch(flag_buf.at[pl.ds(0, NB - 1)], 0).wait_send()
     batch(bias_buf.at[0], 8).wait_send()
-    batch(bias_buf.at[pl.ds(0, na - NZ)], 1).wait_send()
+    batch(bias_buf.at[pl.ds(0, ny - 1)], 1).wait_send()
+    batch(bias_buf.at[pl.ds(0, ny - 1)], 9).wait_send()
     batch(x_buf.at[pl.ds(0, NB - 1)], 2).wait_send()
     batch(live_buf.at[pl.ds(0, na - 1)], 3).wait_send()
     batch(rows_buf.at[pl.ds(0, na - 1)], 4).wait_send()
@@ -427,8 +409,6 @@
         in_specs=[pl.BlockSpec(memory_space=pltpu.HBM)] * 11,
         out_specs=[pl.BlockSpec(memory_space=vmem)] * 2,
         scratch_shapes=[
-            vmem((n, WIDTH), BF16),
-            vmem((1, n), jnp.int32),
             vmem((n, PAIR), BF16),
             vmem((HEADS, PAIR), BF16),
             vmem((WIDTH, 4 * WIDTH), BF16),
@@ -440,8 +420,8 @@
             vmem((2, n, LANES), F32),
             vmem((na, 16, n), BF16),
             vmem((na * 16, n), F32),
-            vmem((NB, na, 2 * WIDTH + n), BF16),
-            vmem((NB, na, 2 * WIDTH + n), BF16),
+            vmem((NB, 1, n), jnp.int32),
+            vmem((NB, na, WIDTH), F32),
             vmem((2 * NB, n), BF16),
             vmem((na, 2 * NB, n), BF16),
             vmem((NB, n, WIDTH), BF16),
@@ -459,8 +439,8 @@
             vmem((NB, n, WIDTH), BF16),
             vmem((NB, HEADS * na, n), F32),
             dma((11,)),
-            dma((9,)),
-            dma((9,)),
+            dma((10,)),
+            dma((10,)),
             dma((NB,)),
         ],
         compiler_params=pltpu.CompilerParams(

time: 47.5 us -> 46.6 us (0.981)
  Pallas kernels: 45.5 us -> 44.6 us
    pallas_call x1, Pallas kernels: 45.5 us -> 44.6 us  [per_device(): pl.pallas_call(functools.partial(kernel, na), out_shape=(vmem((n, WIDTH),...]
where the time goes in v3:
time: 46.6 us; the launch traced here: 46.4 us
  Pallas kernels  44.6 us (96%)
  local copies, waits for them, and re-layouts  1.25 us (3%)
  between operations  0.64 us (1%)
    pallas_call x1, Pallas kernels, per_device(): pl.pallas_call(functools.partial(kernel, na), out_shape=(vmem((n, WIDTH),...  44.6 us
    unnamed x2, local copies, waits for them, and re-layouts  1.25 us

profile of v3, /device:TPU:1, one launch (start us, length us, event | category | flops | bytes accessed | tf_op | source)
XLA Modules:
  0.0 46.4 jit_solution(14706404783815178237)
XLA Ops:
  0.6 44.6 %shard_map.122 = (bf16[128,256]{1,0:T(8,128)(2,1)S(1)}, bf16[1,128,128]{2,1,0:T(8,128)(2,1)S(1)}) custom-call(bf16[1,128,256]{2,1,0:T(8,128)(2,1)} %lineup.1, s32[1,128]{1,0:T(1,128)} %flags.1, bf16[1,128,128]{2,1,0:T(8,128)(2,1)} %couple.1, bf16[8,128]{1,0:T(8,128)(2,1)} %bitcast.7, bf16[256,1024]{1,0:T(8,128)(2,1)} %w_row.1, bf16[256,256]{1,0:T(8,128)(2,1)} %w_row_out.1, ...), custom_call_target="tpu_custom_call" | custom-call | tf_op jit(solution)/shard_map/pallas_call | solution.py:403
  45.2 0.6 %copy.15 = bf16[128,1,256]{2,0,1:T(8,128)(2,1)} copy(bf16[128,1,256]{2,0,1:T(8,128)(2,1)S(1)} %bitcast.4) | data formatting | bytes 131072
  45.8 0.6 %copy.16 = bf16[1,128,128]{2,1,0:T(8,128)(2,1)} copy(bf16[1,128,128]{2,1,0:T(8,128)(2,1)S(1)} %get-tuple-element.7) | data formatting | bytes 65536

commit v4 on v3

--- a/solution.py
+++ b/solution.py
@@ -76,7 +76,6 @@
     bias_wide,
     flag_buf,
     raw_v,
-    live_send,
     live_buf,
     x_buf,
     gated_buf,
@@ -223,12 +222,9 @@
         key_live = flag_buf[seq].astype(F32)
         scores_v[seq] = dot_nt(spread, kv[:, :WIDTH]) + (key_live - 1.0) * MASKED
 
-    batch(flag_buf.at[pl.ds(0, NB - 1)], 0).wait_recv()
     loads[0].wait()
     loads[1].wait()
     project(0)
-    x_copy(lineup.at[0], b_mate(1), 1, b_mate(1)).wait_recv()
-    project(1)
     batch(bias_buf.at[0], 8).wait_recv()
     partner = bias_buf.at[a_mate(1)]
     for r in y_far:
@@ -237,6 +233,15 @@
         slot = b_mate(d * NC)
         x_copy(lineup.at[0], slot, d * NC, b_mate(1)).wait_recv()
         x_copy(x_buf.at[slot], slot, d * NC + 1, b_mate(1)).start()
+
+    batch(flag_buf.at[pl.ds(0, NB - 1)], 0).wait_recv()
+    live8 = jnp.concatenate([flag_buf[k] for k in range(NB)], axis=0).astype(F32)
+    live_buf[a] = jnp.concatenate([live8, live8], axis=0).astype(BF16)
+    for r in [1] + y_far:
+        send(live_buf.at[a], live_buf.at[a], 3, a_mate(r) * NB + b)
+
+    x_copy(lineup.at[0], b_mate(1), 1, b_mate(1)).wait_recv()
+    project(1)
     for d in along_x:
         project(d * NC)
     for d in along_x:
@@ -246,12 +251,6 @@
 
     batch(bias_buf.at[pl.ds(0, ny - 1)], 1).wait_recv()
     batch(bias_buf.at[pl.ds(0, ny - 1)], 9).wait_recv()
-    live8 = jnp.concatenate([flag_buf[k] for k in range(NB)], axis=0).astype(F32)
-    live_send[...] = jnp.concatenate([live8, live8], axis=0).astype(BF16)
-    for r in a_far:
-        send(live_send, live_buf.at[a], 3, a_mate(r) * NB + b)
-    live_buf[a] = live_send[...]
-
     bias_wide[...] = bias_buf[...].astype(F32).reshape(na * 16, n)
     score_bias = jnp.concatenate(
         [bias_wide[pl.ds(h, na, stride=16), :] for h in range(HEADS)], axis=0
@@ -286,7 +285,12 @@
         send(rows_send.at[mate], rows_buf.at[a], 4, mate * NB + b)
     rows_buf[a] = rows_send[a]
 
-    batch(live_buf.at[pl.ds(0, na - 1)], 3).wait_recv()
+    batch(live_buf.at[pl.ds(0, ny)], 3).wait_recv()
+    partner = live_buf.at[a_mate(1)]
+    for r in y_far:
+        send(partner, partner, 10, a_mate(r) * NB + b)
+
+    batch(live_buf.at[pl.ds(0, ny - 1)], 10).wait_recv()
     live_all = live_buf[...].astype(F32)[:, :NB].reshape(n, n).astype(BF16)
     own = (iota((16, n), 1) == me).astype(BF16)
     own_live = dot_nt(own, live_all)[:1]
@@ -385,7 +389,8 @@
     batch(bias_buf.at[pl.ds(0, ny - 1)], 1).wait_send()
     batch(bias_buf.at[pl.ds(0, ny - 1)], 9).wait_send()
     batch(x_buf.at[pl.ds(0, NB - 1)], 2).wait_send()
-    batch(live_buf.at[pl.ds(0, na - 1)], 3).wait_send()
+    batch(live_buf.at[pl.ds(0, ny)], 3).wait_send()
+    batch(live_buf.at[pl.ds(0, ny - 1)], 10).wait_send()
     batch(rows_buf.at[pl.ds(0, na - 1)], 4).wait_send()
     batch(left_buf.at[pl.ds(0, ne - 1)], 5).wait_send()
     batch(right_buf.at[pl.ds(0, NF - 1)], 6).wait_send()
@@ -422,7 +427,6 @@
             vmem((na * 16, n), F32),
             vmem((NB, 1, n), jnp.int32),
             vmem((NB, na, WIDTH), F32),
-            vmem((2 * NB, n), BF16),
             vmem((na, 2 * NB, n), BF16),
             vmem((NB, n, WIDTH), BF16),
             vmem((NB, na, WIDTH), BF16),
@@ -439,8 +443,8 @@
             vmem((NB, n, WIDTH), BF16),
             vmem((NB, HEADS * na, n), F32),
             dma((11,)),
-            dma((10,)),
-            dma((10,)),
+            dma((11,)),
+            dma((11,)),
             dma((NB,)),
         ],
         compiler_params=pltpu.CompilerParams(

time: 46.6 us -> 45.1 us (0.968)
  Pallas kernels: 44.6 us -> 43.1 us
    pallas_call x1, Pallas kernels: 44.6 us -> 43.1 us  [per_device(): pl.pallas_call(functools.partial(kernel, na), out_shape=(vmem((n, WIDTH),...]
where the time goes in v4:
time: 45.1 us; the launch traced here: 45 us
  Pallas kernels  43.1 us (96%)
  local copies, waits for them, and re-layouts  1.25 us (3%)
  between operations  0.64 us (1%)
    pallas_call x1, Pallas kernels, per_device(): pl.pallas_call(functools.partial(kernel, na), out_shape=(vmem((n, WIDTH),...  43.1 us
    unnamed x2, local copies, waits for them, and re-layouts  1.25 us

profile of v4, /device:TPU:1, one launch (start us, length us, event | category | flops | bytes accessed | tf_op | source)
XLA Modules:
  0.0 45.0 jit_solution(6499535538315631053)
XLA Ops:
  0.6 43.1 %shard_map.122 = (bf16[128,256]{1,0:T(8,128)(2,1)S(1)}, bf16[1,128,128]{2,1,0:T(8,128)(2,1)S(1)}) custom-call(bf16[1,128,256]{2,1,0:T(8,128)(2,1)} %lineup.1, s32[1,128]{1,0:T(1,128)} %flags.1, bf16[1,128,128]{2,1,0:T(8,128)(2,1)} %couple.1, bf16[8,128]{1,0:T(8,128)(2,1)} %bitcast.7, bf16[256,1024]{1,0:T(8,128)(2,1)} %w_row.1, bf16[256,256]{1,0:T(8,128)(2,1)} %w_row_out.1, ...), custom_call_target="tpu_custom_call" | custom-call | tf_op jit(solution)/shard_map/pallas_call | solution.py:408
  43.7 0.6 %copy.15 = bf16[128,1,256]{2,0,1:T(8,128)(2,1)} copy(bf16[128,1,256]{2,0,1:T(8,128)(2,1)S(1)} %bitcast.4) | data formatting | bytes 131072
  44.4 0.6 %copy.16 = bf16[1,128,128]{2,1,0:T(8,128)(2,1)} copy(bf16[1,128,128]{2,1,0:T(8,128)(2,1)S(1)} %get-tuple-element.7) | data formatting | bytes 65536

commit v5 on v4

--- a/solution.py
+++ b/solution.py
@@ -17,7 +17,6 @@
 MASKED = 1e9
 NZ, NX, NC = 2, 4, 2
 NB = NX * NC
-NF = NZ * NX
 
 F32 = jnp.float32
 BF16 = jnp.bfloat16
@@ -82,8 +81,10 @@
     rows_wide,
     rows_send,
     rows_buf,
+    left_v,
     left_buf,
     right_buf,
+    align_v,
     products,
     final_rep,
     update_send,
@@ -98,11 +99,9 @@
 ):
     n = na * NB
     ny = na // NZ
-    ne = ny * NC
     me = lax.axis_index("dap")
     a, b = me // NB, me % NB
     y, z, x_at, c = a // NZ, a % NZ, b // NC, b % NC
-    e, f = c * ny + y, z * NX + x_at
 
     def around(size, r):
         return min(r, size - r)
@@ -113,19 +112,8 @@
     def a_mate(r):
         return (y + r // NZ) % ny * NZ + (z + r) % NZ
 
-    def e_mate(r):
-        return (c + r // ny) % NC * ny + (y + r) % ny
-
-    def f_mate(r):
-        return (z + r // NX) % NZ * NX + (x_at + r) % NX
-
-    def from_ef(e_at, f_at):
-        return ((e_at % ny * NZ + f_at // NX) * NX + f_at % NX) * NC + e_at // ny
-
     b_far = sorted(range(1, NB), key=lambda r: -around(NX, r // NC) * 2 - r % NC)
     a_far = sorted(range(1, na), key=lambda r: -around(ny, r // NZ) - 4 * (r % NZ))
-    e_far = sorted(range(1, ne), key=lambda r: -around(ny, r % ny) * 2 - r // ny)
-    f_far = sorted(range(1, NF), key=lambda r: -around(NX, r % NX) - 4 * (r // NX))
     y_far = [r for r in a_far if r % NZ == 0]
 
     barrier = pltpu.get_barrier_semaphore()
@@ -198,8 +186,9 @@
     x_copy(lineup.at[0], b, 1, b_mate(1)).start()
 
     loads[10].wait()
+    products[...] = w_final_v[...].astype(F32)
     for k in range(OUTER):
-        part = w_final_v[k * OUTER : (k + 1) * OUTER, :]
+        part = products[pl.ds(k, OUTER, stride=OUTER), :].astype(BF16)
         for copy in range(4):
             at = (k * 4 + copy) * OUTER
             final_rep[at : at + OUTER, :] = part
@@ -282,8 +271,9 @@
         ).astype(BF16)
     for r in a_far:
         mate = a_mate(r)
-        send(rows_send.at[mate], rows_buf.at[a], 4, mate * NB + b)
-    rows_buf[a] = rows_send[a]
+        both = rows_send.at[pl.ds(mate // NZ * NZ, NZ)]
+        send(both, rows_buf.at[a], 4, mate * NB + b)
+    rows_buf[a] = rows_send[pl.ds(y * NZ, NZ)]
 
     batch(live_buf.at[pl.ds(0, ny)], 3).wait_recv()
     partner = live_buf.at[a_mate(1)]
@@ -292,16 +282,12 @@
 
     batch(live_buf.at[pl.ds(0, ny - 1)], 10).wait_recv()
     live_all = live_buf[...].astype(F32)[:, :NB].reshape(n, n).astype(BF16)
-    own = (iota((16, n), 1) == me).astype(BF16)
-    own_live = dot_nt(own, live_all)[:1]
+    both = (y * NZ + iota((NZ * 8, n), 0) // 8) * NB + b
+    both_live = dot_nt((iota((NZ * 8, n), 1) == both).astype(BF16), live_all)
+    own_live = [both_live[k * 8 : k * 8 + 1] for k in range(NZ)]
     pick = (NB * na, n)
-    tile_e, tile_f = iota(pick, 0) % ne, iota(pick, 0) // ne
-
-    def place(y_at, z_at, x_of, core):
-        return ((y_at * NZ + z_at) * NX + x_of) * NC + core
-
-    pick_i = (iota(pick, 1) == place(tile_e % ny, z, x_at, tile_e // ny)).astype(BF16)
-    pick_j = (iota(pick, 1) == place(y, tile_f // NX, tile_f % NX, c)).astype(BF16)
+    pick_i = (iota(pick, 1) == a * NB + iota(pick, 0) // na).astype(BF16)
+    pick_j = (iota(pick, 1) == iota(pick, 0) % na * NB + b).astype(BF16)
     counts = jnp.sum(
         dot_nt(pick_i, live_all) * dot_nt(pick_j, live_all), axis=-1, keepdims=True
     )
@@ -318,51 +304,71 @@
     batch(rows_buf.at[pl.ds(0, na - 1)], 4).wait_recv()
     arrived = rows_buf[...].astype(F32)
     column = jnp.concatenate(
-        [arrived[:, :NB].reshape(n, LANES), arrived[:, NB:].reshape(n, LANES)], axis=1
+        [
+            jnp.concatenate(
+                [
+                    arrived[:, k, :NB].reshape(n, LANES),
+                    arrived[:, k, NB:].reshape(n, LANES),
+                ],
+                axis=1,
+            )
+            for k in range(NZ)
+        ],
+        axis=0,
     )
     mapped = dot(normed(column), w_col_v[...])
     queries = (mapped[:, :WIDTH] * HEAD_DIM**-0.5).astype(BF16)
     keys = mapped[:, WIDTH : 2 * WIDTH].astype(BF16)
     values = mapped[:, 2 * WIDTH : 3 * WIDTH].astype(BF16)
-    key_bias = (own_live - 1.0) * MASKED
-    expos, spread_values = [], []
-    for h in range(HEADS):
-        scores = dot_nt(jnp.where(col_head == h, queries, 0), keys) + key_bias
-        expos.append(jnp.exp(scores - jnp.max(scores, axis=-1, keepdims=True)).astype(BF16))
-        spread_values.append(jnp.where(col_head == h, values, 0))
-    expo = jnp.concatenate(expos, axis=1)
-    mixed = dot(expo, jnp.concatenate(spread_values, axis=0)) / dot(expo, ones_bd)
+    mixed, expos = [], []
+    for k in range(NZ):
+        rows = slice(k * n, (k + 1) * n)
+        key_bias = (own_live[k] - 1.0) * MASKED
+        parts, spread_values = [], []
+        for h in range(HEADS):
+            scores = dot_nt(jnp.where(col_head == h, queries[rows], 0), keys[rows]) + key_bias
+            parts.append(jnp.exp(scores - jnp.max(scores, axis=-1, keepdims=True)).astype(BF16))
+            spread_values.append(jnp.where(col_head == h, values[rows], 0))
+        expos.append(jnp.concatenate(parts, axis=1))
+        mixed.append(dot(expos[k], jnp.concatenate(spread_values, axis=0)))
+    mixed = jnp.concatenate(mixed, axis=0) / dot(jnp.concatenate(expos, axis=0), ones_bd)
     gated = (jax.nn.sigmoid(mapped[:, 3 * WIDTH :]) * mixed).astype(BF16)
     updated = (column + dot(gated, w_col_out_v[...])).astype(BF16)
-    align_out[...] = updated
-
-    outer = (dot_nt(w_outer_v[...], normed(updated.astype(F32))) * own_live).astype(BF16)
-    left_buf[e] = outer[:OUTER]
-    right_buf[f] = outer[OUTER:]
-    for r in f_far:
-        send(right_buf.at[f], right_buf.at[f], 6, from_ef(e, f_mate(r)))
-    for r in e_far:
-        send(left_buf.at[e], left_buf.at[e], 5, from_ef(e_mate(r), f))
-    batch(left_buf.at[pl.ds(0, ne - 1)], 5).wait_recv()
-    batch(right_buf.at[pl.ds(0, NF - 1)], 6).wait_recv()
-    lefts = left_buf[...].reshape(ne * OUTER, n)
-    rights = right_buf[...].reshape(NF * OUTER, n)
-    product = dot_nt(lefts, rights)
-    depth = ne * OUTER
+
+    outer = dot_nt(w_outer_v[...], normed(updated.astype(F32)))
+    outer = (outer * jnp.concatenate(own_live, axis=1)).astype(BF16)
+    for k in range(NZ):
+        left_v[k] = outer[:OUTER, k * n : (k + 1) * n]
+        right_buf[y * NZ + k] = outer[OUTER:, k * n : (k + 1) * n]
+    left_buf[b] = left_v[z]
+    rights = right_buf.at[pl.ds(y * NZ, NZ)]
+    for r in y_far:
+        send(rights, rights, 6, a_mate(r) * NB + b)
+    for r in b_far:
+        send(left_buf.at[b], left_buf.at[b], 5, a * NB + b_mate(r))
+    align_v[...] = updated.reshape(NZ, n, WIDTH)
+    align_out[...] = align_v[z]
+    wide[...] = couple_v[...].astype(F32)
+    batch(left_buf.at[pl.ds(0, NB - 1)], 5).wait_recv()
+    batch(right_buf.at[pl.ds(0, na - NZ)], 6).wait_recv()
+    lefts = left_buf[...].reshape(NB * OUTER, n)
+    rights = right_buf[...].reshape(na * OUTER, n)
+    product = dot_nt(rights, lefts)
+    depth = na * OUTER
     products[pl.ds(0, depth), :] = product[:, :LANES]
     products[pl.ds(depth, depth), :] = product[:, LANES:]
-    quarter = iota((ne, LANES), 1) // OUTER
+    quarter = iota((na, LANES), 1) // OUTER
     step = 8
     total = None
     for first in range(0, OUTER, step):
         slabs = []
         for k in range(first, first + step):
             tiles = [
-                products[pl.ds(t * depth + k, ne, stride=OUTER), :].astype(BF16) for t in range(2)
+                products[pl.ds(t * depth + k, na, stride=OUTER), :].astype(BF16) for t in range(2)
             ]
             slabs.append(
                 jnp.concatenate(
-                    [jnp.where(quarter == j % 4, tiles[j // 4], 0) for j in range(NF)], axis=0
+                    [jnp.where(quarter == i % 4, tiles[i // 4], 0) for i in range(NB)], axis=0
                 )
             )
         term = dot(
@@ -370,19 +376,16 @@
             final_rep[pl.ds(first * LANES, step * LANES), :],
         )
         total = term if total is None else total + term
-    rows_wide[0] = total / counts
-    for k in range(ne):
-        update_send[k] = rows_wide[0, pl.ds(k, NF, stride=ne), :]
-    for r in e_far:
-        mate = e_mate(r)
-        send(update_send.at[mate], update_buf.at[e], 7, from_ef(mate, f))
-    update_buf[e] = update_send[e]
-    wide[1] = couple_v[...].astype(F32)
-    batch(update_send.at[pl.ds(0, ne - 1)], 7).wait_recv()
-    for k in range(ne):
-        at = pl.ds(k % ny * (NF * NC) + k // ny, NF, stride=NC)
-        wide[1, at, :] = wide[1, at, :] + update_buf[k]
-    pair_out[0] = wide[1].astype(BF16)
+    update_send[...] = (total / counts).reshape(NB, na, PAIR)
+    for r in b_far:
+        mate = b_mate(r)
+        send(update_send.at[mate], update_buf.at[b], 7, a * NB + mate)
+    update_buf[b] = update_send[b]
+    batch(update_send.at[pl.ds(0, NB - 1)], 7).wait_recv()
+    for k in range(NB):
+        at = pl.ds(k, na, stride=NB)
+        wide[at, :] = wide[at, :] + update_buf[k]
+    pair_out[0] = wide[...].astype(BF16)
 
     batch(flag_buf.at[pl.ds(0, NB - 1)], 0).wait_send()
     batch(bias_buf.at[0], 8).wait_send()
@@ -392,9 +395,9 @@
     batch(live_buf.at[pl.ds(0, ny)], 3).wait_send()
     batch(live_buf.at[pl.ds(0, ny - 1)], 10).wait_send()
     batch(rows_buf.at[pl.ds(0, na - 1)], 4).wait_send()
-    batch(left_buf.at[pl.ds(0, ne - 1)], 5).wait_send()
-    batch(right_buf.at[pl.ds(0, NF - 1)], 6).wait_send()
-    batch(update_send.at[pl.ds(0, ne - 1)], 7).wait_send()
+    batch(left_buf.at[pl.ds(0, NB - 1)], 5).wait_send()
+    batch(right_buf.at[pl.ds(0, na - NZ)], 6).wait_send()
+    batch(update_send.at[pl.ds(0, NB - 1)], 7).wait_send()
 
 
 def per_device(
@@ -402,7 +405,6 @@
 ):
     n = lineup.shape[1]
     na = n // NB
-    ne = na // NZ * NC
     vmem = pltpu.VMEM
     dma = pltpu.SemaphoreType.DMA
     align, pair = pl.pallas_call(
@@ -422,7 +424,7 @@
             vmem((WIDTH, WIDTH), BF16),
             vmem((2 * OUTER, WIDTH), BF16),
             vmem((OUTER * OUTER, PAIR), BF16),
-            vmem((2, n, LANES), F32),
+            vmem((n, PAIR), F32),
             vmem((na, 16, n), BF16),
             vmem((na * 16, n), F32),
             vmem((NB, 1, n), jnp.int32),
@@ -432,13 +434,15 @@
             vmem((NB, na, WIDTH), BF16),
             vmem((2, n, LANES), F32),
             vmem((na, 2 * NB, LANES), BF16),
-            vmem((na, 2 * NB, LANES), BF16),
-            vmem((ne, OUTER, n), BF16),
-            vmem((NF, OUTER, n), BF16),
+            vmem((na, NZ, 2 * NB, LANES), BF16),
+            vmem((NZ, OUTER, n), BF16),
+            vmem((NB, OUTER, n), BF16),
+            vmem((na, OUTER, n), BF16),
+            vmem((NZ, n, WIDTH), BF16),
             vmem((OUTER * OUTER, LANES), F32),
             vmem((OUTER * LANES, PAIR), BF16),
-            vmem((ne, NF, PAIR), F32),
-            vmem((ne, NF, PAIR), F32),
+            vmem((NB, na, PAIR), F32),
+            vmem((NB, na, PAIR), F32),
             vmem((NB, na, WIDTH), F32),
             vmem((NB, n, WIDTH), BF16),
             vmem((NB, HEADS * na, n), F32),

time: 45.1 us -> 44.5 us (0.987)
  Pallas kernels: 43.1 us -> 42.5 us
    pallas_call x1, Pallas kernels: 43.1 us -> 42.5 us  [per_device(): pl.pallas_call(functools.partial(kernel, na), out_shape=(vmem((n, WIDTH),...]
where the time goes in v5:
time: 44.5 us; the launch traced here: 44.4 us
  Pallas kernels  42.5 us (96%)
  local copies, waits for them, and re-layouts  1.25 us (3%)
  between operations  0.64 us (1%)
    pallas_call x1, Pallas kernels, per_device(): pl.pallas_call(functools.partial(kernel, na), out_shape=(vmem((n, WIDTH),...  42.5 us
    unnamed x2, local copies, waits for them, and re-layouts  1.25 us

profile of v5, /device:TPU:1, one launch (start us, length us, event | category | flops | bytes accessed | tf_op | source)
XLA Modules:
  0.0 44.4 jit_solution(2565169677799172209)
XLA Ops:
  0.6 42.5 %shard_map.122 = (bf16[128,256]{1,0:T(8,128)(2,1)S(1)}, bf16[1,128,128]{2,1,0:T(8,128)(2,1)S(1)}) custom-call(bf16[1,128,256]{2,1,0:T(8,128)(2,1)} %lineup.1, s32[1,128]{1,0:T(1,128)} %flags.1, bf16[1,128,128]{2,1,0:T(8,128)(2,1)} %couple.1, bf16[8,128]{1,0:T(8,128)(2,1)} %bitcast.7, bf16[256,1024]{1,0:T(8,128)(2,1)} %w_row.1, bf16[256,256]{1,0:T(8,128)(2,1)} %w_row_out.1, ...), custom_call_target="tpu_custom_call" | custom-call | tf_op jit(solution)/shard_map/pallas_call | solution.py:410
  43.2 0.6 %copy.15 = bf16[128,1,256]{2,0,1:T(8,128)(2,1)} copy(bf16[128,1,256]{2,0,1:T(8,128)(2,1)S(1)} %bitcast.4) | data formatting | bytes 131072
  43.8 0.6 %copy.16 = bf16[1,128,128]{2,1,0:T(8,128)(2,1)} copy(bf16[1,128,128]{2,1,0:T(8,128)(2,1)S(1)} %get-tuple-element.7) | data formatting | bytes 65536

commit v6 on v5

--- a/solution.py
+++ b/solution.py
@@ -43,8 +43,8 @@
 
 
 def head_mask(rows_per_head):
-    shape = (HEADS * rows_per_head, WIDTH)
-    return iota(shape, 0) // rows_per_head == iota(shape, 1) // HEAD_DIM
+    shape = (NZ * HEADS * rows_per_head, WIDTH)
+    return iota(shape, 0) // rows_per_head % HEADS == iota(shape, 1) // HEAD_DIM
 
 
 def kernel(
@@ -77,7 +77,6 @@
     raw_v,
     live_buf,
     x_buf,
-    gated_buf,
     rows_wide,
     rows_send,
     rows_buf,
@@ -92,6 +91,7 @@
     gates_v,
     values_v,
     scores_v,
+    round_sem,
     in_sems,
     send_sems,
     recv_sems,
@@ -115,10 +115,6 @@
     b_far = sorted(range(1, NB), key=lambda r: -around(NX, r // NC) * 2 - r % NC)
     a_far = sorted(range(1, na), key=lambda r: -around(ny, r // NZ) - 4 * (r % NZ))
     y_far = [r for r in a_far if r % NZ == 0]
-
-    barrier = pltpu.get_barrier_semaphore()
-    for mate in [a_mate(r) * NB + b for r in [1] + y_far] + [a * NB + b_mate(r) for r in b_far]:
-        pl.semaphore_signal(barrier, inc=1, device_id={"dap": mate}, device_id_type=MESH)
 
     pairs = (
         (lineup.at[0], x_buf.at[b]),
@@ -134,8 +130,14 @@
         (w_final, w_final_v),
     )
     loads = [pltpu.make_async_copy(src, dst, in_sems.at[k]) for k, (src, dst) in enumerate(pairs)]
-    for k in (2, 3, 0, 1, 4, 5, 6, 7, 8, 9, 10):
-        loads[k].start()
+    loads[2].start()
+    loads[3].start()
+
+    beside = [a_mate(r) * NB + b for r in y_far if around(ny, r // NZ) <= 2]
+    barrier = pltpu.get_barrier_semaphore()
+    greeted = [a_mate(1) * NB + b] + beside + [a * NB + b_mate(r) for r in b_far]
+    for mate in greeted:
+        pl.semaphore_signal(barrier, inc=1, device_id={"dap": mate}, device_id_type=MESH)
 
     def send(src, dst, phase, device):
         copy = pltpu.make_async_remote_copy(
@@ -170,20 +172,27 @@
 
     loads[2].wait()
     loads[3].wait()
+    for k in (0, 1, 4, 5, 6, 7, 8, 9, 10):
+        loads[k].start()
     bias = dot_nt(offset_v[...], normed(couple_v[...].astype(F32)))
     bias_buf[a] = jnp.concatenate([bias, jnp.zeros_like(bias)], axis=0).astype(BF16)
 
-    pl.semaphore_wait(barrier, NB + ny - 1)
+    pl.semaphore_wait(barrier, len(greeted))
 
     send(bias_buf.at[a], bias_buf.at[a], 8, a_mate(1) * NB + b)
-    for r in y_far:
-        send(bias_buf.at[a], bias_buf.at[a], 1, a_mate(r) * NB + b)
     for r in b_far:
         send(flags, flag_buf.at[b], 0, a * NB + b_mate(r))
     along_x = sorted(range(1, NX), key=lambda d: around(NX, d))
     for d in along_x:
         x_copy(lineup.at[0], b, (NX - d) % NX * NC, b_mate(d * NC)).start()
     x_copy(lineup.at[0], b, 1, b_mate(1)).start()
+
+    assert ny <= 9
+    for mate in beside:
+        pl.semaphore_signal(round_sem, inc=1, device_id={"dap": mate}, device_id_type=MESH)
+    pl.semaphore_wait(round_sem, len(beside))
+    for r in y_far:
+        send(bias_buf.at[a], bias_buf.at[a], 1, a_mate(r) * NB + b)
 
     loads[10].wait()
     products[...] = w_final_v[...].astype(F32)
@@ -194,8 +203,10 @@
             final_rep[at : at + OUTER, :] = part
 
     loads[4].wait()
-    own_head = head_mask(na)
-    pick_query = (iota((na, n), 1) == iota((na, n), 0) * NB + b).astype(BF16)
+    own_head = head_mask(ny)
+    at_query = iota((na, n), 0)
+    at_query = (at_query % ny * NZ + (z + at_query // ny) % NZ) * NB + b
+    pick_query = (iota((na, n), 1) == at_query).astype(BF16)
 
     def project(r):
         seq = b_mate(r)
@@ -203,11 +214,12 @@
         x_norm = normed(x.astype(F32))
         raw_v[seq] = dot(pick_query, x)
         query_in = dot(pick_query, x_norm).astype(BF16)
-        query = (dot(query_in, w_row_v[:, :WIDTH]) * HEAD_DIM**-0.5).astype(BF16)
+        query = (dot(query_in, w_row_v[:, :WIDTH]) * HEAD_DIM**-0.5).astype(BF16).astype(F32)
         gates_v[seq] = jax.nn.sigmoid(dot(query_in, w_row_v[:, 3 * WIDTH :]))
         kv = dot(x_norm, w_row_v[:, WIDTH : 3 * WIDTH]).astype(BF16)
         values_v[seq] = kv[:, WIDTH:]
-        spread = jnp.where(own_head, jnp.concatenate([query] * HEADS, axis=0), 0)
+        spread = [query[k * ny : (k + 1) * ny] for k in range(NZ) for _ in range(HEADS)]
+        spread = jnp.where(own_head, jnp.concatenate(spread, axis=0), 0).astype(BF16)
         key_live = flag_buf[seq].astype(F32)
         scores_v[seq] = dot_nt(spread, kv[:, :WIDTH]) + (key_live - 1.0) * MASKED
 
@@ -238,37 +250,46 @@
     for d in along_x:
         project(d * NC + 1)
 
+    lane_head = iota((ny, WIDTH), 1) // HEAD_DIM
+    ones = jnp.ones((n, LANES), BF16)
+    loads[5].wait()
+
+    def finish(k):
+        z_at = (z + k) % NZ
+        for row in range(ny):
+            tile = bias_buf[row * NZ + z_at].astype(F32)
+            bias_wide[k, row * HEADS : (row + 1) * HEADS, :] = tile[:HEADS]
+        score_bias = jnp.concatenate(
+            [bias_wide[k, pl.ds(h, ny, stride=HEADS), :] for h in range(HEADS)], axis=0
+        )
+        gated = []
+        for seq in range(NB):
+            scores = scores_v[seq, k * HEADS * ny : (k + 1) * HEADS * ny, :] + score_bias
+            expo = jnp.exp(scores - jnp.max(scores, axis=-1, keepdims=True)).astype(BF16)
+            mixed = dot(expo, values_v[seq])
+            total = dot(expo, ones)
+            top, bottom = mixed[:ny], jnp.concatenate([total[:ny]] * 2, axis=1)
+            for h in range(1, HEADS):
+                rows = slice(h * ny, (h + 1) * ny)
+                top = jnp.where(lane_head == h, mixed[rows], top)
+                bottom = jnp.where(
+                    lane_head == h, jnp.concatenate([total[rows]] * 2, axis=1), bottom
+                )
+            gated.append(gates_v[seq, k * ny : (k + 1) * ny, :] * (top / bottom))
+        grown = dot(jnp.concatenate(gated, axis=0).astype(BF16), w_row_out_v[...])
+        raw = [raw_v[seq, k * ny : (k + 1) * ny, :] for seq in range(NB)]
+        grown = jnp.concatenate(raw, axis=0) + grown
+        rows_wide[k, 0] = grown[:, :LANES]
+        rows_wide[k, 1] = grown[:, LANES:]
+        for row in range(ny):
+            rows_send[row * NZ + z_at] = jnp.concatenate(
+                [rows_wide[k, half, pl.ds(row, NB, stride=ny), :] for half in range(2)], axis=0
+            ).astype(BF16)
+
     batch(bias_buf.at[pl.ds(0, ny - 1)], 1).wait_recv()
+    finish(0)
     batch(bias_buf.at[pl.ds(0, ny - 1)], 9).wait_recv()
-    bias_wide[...] = bias_buf[...].astype(F32).reshape(na * 16, n)
-    score_bias = jnp.concatenate(
-        [bias_wide[pl.ds(h, na, stride=16), :] for h in range(HEADS)], axis=0
-    )
-    lane_head = iota((na, WIDTH), 1) // HEAD_DIM
-    ones = jnp.ones((n, LANES), BF16)
-    for seq in range(NB):
-        scores = scores_v[seq] + score_bias
-        expo = jnp.exp(scores - jnp.max(scores, axis=-1, keepdims=True)).astype(BF16)
-        mixed = dot(expo, values_v[seq])
-        total = dot(expo, ones)
-        top, bottom = mixed[:na], jnp.concatenate([total[:na]] * 2, axis=1)
-        for h in range(1, HEADS):
-            rows = slice(h * na, (h + 1) * na)
-            top = jnp.where(lane_head == h, mixed[rows], top)
-            bottom = jnp.where(
-                lane_head == h, jnp.concatenate([total[rows]] * 2, axis=1), bottom
-            )
-        gated_buf[seq] = (gates_v[seq] * (top / bottom)).astype(BF16)
-
-    loads[5].wait()
-    grown = dot(gated_buf[...].reshape(NB * na, WIDTH), w_row_out_v[...])
-    grown = raw_v[...].reshape(NB * na, WIDTH) + grown
-    rows_wide[0] = grown[:, :LANES]
-    rows_wide[1] = grown[:, LANES:]
-    for k in range(na):
-        rows_send[k] = jnp.concatenate(
-            [rows_wide[h, pl.ds(k, NB, stride=na), :] for h in range(2)], axis=0
-        ).astype(BF16)
+    finish(1)
     for r in a_far:
         mate = a_mate(r)
         both = rows_send.at[pl.ds(mate // NZ * NZ, NZ)]
@@ -381,12 +402,6 @@
         mate = b_mate(r)
         send(update_send.at[mate], update_buf.at[b], 7, a * NB + mate)
     update_buf[b] = update_send[b]
-    batch(update_send.at[pl.ds(0, NB - 1)], 7).wait_recv()
-    for k in range(NB):
-        at = pl.ds(k, na, stride=NB)
-        wide[at, :] = wide[at, :] + update_buf[k]
-    pair_out[0] = wide[...].astype(BF16)
-
     batch(flag_buf.at[pl.ds(0, NB - 1)], 0).wait_send()
     batch(bias_buf.at[0], 8).wait_send()
     batch(bias_buf.at[pl.ds(0, ny - 1)], 1).wait_send()
@@ -398,6 +413,11 @@
     batch(left_buf.at[pl.ds(0, NB - 1)], 5).wait_send()
     batch(right_buf.at[pl.ds(0, na - NZ)], 6).wait_send()
     batch(update_send.at[pl.ds(0, NB - 1)], 7).wait_send()
+    batch(update_send.at[pl.ds(0, NB - 1)], 7).wait_recv()
+    for k in range(NB):
+        at = pl.ds(k, na, stride=NB)
+        wide[at, :] = wide[at, :] + update_buf[k]
+    pair_out[0] = wide[...].astype(BF16)
 
 
 def per_device(
@@ -426,13 +446,12 @@
             vmem((OUTER * OUTER, PAIR), BF16),
             vmem((n, PAIR), F32),
             vmem((na, 16, n), BF16),
-            vmem((na * 16, n), F32),
+            vmem((NZ, na // NZ * HEADS, n), F32),
             vmem((NB, 1, n), jnp.int32),
             vmem((NB, na, WIDTH), F32),
             vmem((na, 2 * NB, n), BF16),
             vmem((NB, n, WIDTH), BF16),
-            vmem((NB, na, WIDTH), BF16),
-            vmem((2, n, LANES), F32),
+            vmem((NZ, 2, na // NZ * NB, LANES), F32),
             vmem((na, 2 * NB, LANES), BF16),
             vmem((na, NZ, 2 * NB, LANES), BF16),
             vmem((NZ, OUTER, n), BF16),
@@ -446,6 +465,7 @@
             vmem((NB, na, WIDTH), F32),
             vmem((NB, n, WIDTH), BF16),
             vmem((NB, HEADS * na, n), F32),
+            pltpu.SemaphoreType.REGULAR,
             dma((11,)),
             dma((11,)),
             dma((11,)),

time: 44.5 us -> 44.4 us (level)
  no operation moved by 1% of the time
where the time goes in v6:
time: 44.4 us; the launch traced here: 44.2 us
  Pallas kernels  42.3 us (95%)
  local copies, waits for them, and re-layouts  1.25 us (3%)
  between operations  0.64 us (1%)
    pallas_call x1, Pallas kernels, per_device(): pl.pallas_call(functools.partial(kernel, na), out_shape=(vmem((n, WIDTH),...  42.3 us
    unnamed x2, local copies, waits for them, and re-layouts  1.25 us

profile of v6, /device:TPU:1, one launch (start us, length us, event | category | flops | bytes accessed | tf_op | source)
XLA Modules:
  0.0 44.2 jit_solution(2123188964299320339)
XLA Ops:
  0.6 42.3 %shard_map.122 = (bf16[128,256]{1,0:T(8,128)(2,1)S(1)}, bf16[1,128,128]{2,1,0:T(8,128)(2,1)S(1)}) custom-call(bf16[1,128,256]{2,1,0:T(8,128)(2,1)} %lineup.1, s32[1,128]{1,0:T(1,128)} %flags.1, bf16[1,128,128]{2,1,0:T(8,128)(2,1)} %couple.1, bf16[8,128]{1,0:T(8,128)(2,1)} %bitcast.7, bf16[256,1024]{1,0:T(8,128)(2,1)} %w_row.1, bf16[256,256]{1,0:T(8,128)(2,1)} %w_row_out.1, ...), custom_call_target="tpu_custom_call" | custom-call | tf_op jit(solution)/shard_map/pallas_call | solution.py:430
  43.0 0.6 %copy.15 = bf16[128,1,256]{2,0,1:T(8,128)(2,1)} copy(bf16[128,1,256]{2,0,1:T(8,128)(2,1)S(1)} %bitcast.4) | data formatting | bytes 131072
  43.6 0.6 %copy.16 = bf16[1,128,128]{2,1,0:T(8,128)(2,1)} copy(bf16[1,128,128]{2,1,0:T(8,128)(2,1)S(1)} %get-tuple-element.7) | data formatting | bytes 65536

commit v7 on v6

--- a/solution.py
+++ b/solution.py
@@ -374,33 +374,33 @@
     batch(right_buf.at[pl.ds(0, na - NZ)], 6).wait_recv()
     lefts = left_buf[...].reshape(NB * OUTER, n)
     rights = right_buf[...].reshape(na * OUTER, n)
-    product = dot_nt(rights, lefts)
     depth = na * OUTER
-    products[pl.ds(0, depth), :] = product[:, :LANES]
-    products[pl.ds(depth, depth), :] = product[:, LANES:]
     quarter = iota((na, LANES), 1) // OUTER
     step = 8
-    total = None
-    for first in range(0, OUTER, step):
-        slabs = []
-        for k in range(first, first + step):
-            tiles = [
-                products[pl.ds(t * depth + k, na, stride=OUTER), :].astype(BF16) for t in range(2)
-            ]
-            slabs.append(
-                jnp.concatenate(
-                    [jnp.where(quarter == i % 4, tiles[i // 4], 0) for i in range(NB)], axis=0
+    for t in range(NB // 4):
+        at = t * depth
+        products[at : at + depth, :] = dot_nt(rights, lefts[t * LANES : (t + 1) * LANES])
+        total = None
+        for first in range(0, OUTER, step):
+            slabs = []
+            for k in range(first, first + step):
+                tile = products[pl.ds(at + k, na, stride=OUTER), :].astype(BF16)
+                slabs.append(
+                    jnp.concatenate([jnp.where(quarter == i, tile, 0) for i in range(4)], axis=0)
                 )
+            term = dot(
+                jnp.concatenate(slabs, axis=1),
+                final_rep[pl.ds(first * LANES, step * LANES), :],
             )
-        term = dot(
-            jnp.concatenate(slabs, axis=1),
-            final_rep[pl.ds(first * LANES, step * LANES), :],
-        )
-        total = term if total is None else total + term
-    update_send[...] = (total / counts).reshape(NB, na, PAIR)
-    for r in b_far:
-        mate = b_mate(r)
-        send(update_send.at[mate], update_buf.at[b], 7, a * NB + mate)
+            total = term if total is None else total + term
+        rows = slice(t * 4 * na, (t + 1) * 4 * na)
+        update_send[t * 4 : (t + 1) * 4] = (total / counts[rows]).reshape(4, na, PAIR)
+        for mate in range(t * 4, (t + 1) * 4):
+
+            @pl.when(b != mate)
+            def _():
+                send(update_send.at[mate], update_buf.at[b], 7, a * NB + mate)
+
     update_buf[b] = update_send[b]
     batch(flag_buf.at[pl.ds(0, NB - 1)], 0).wait_send()
     batch(bias_buf.at[0], 8).wait_send()

time: 44.4 us -> 44.4 us (level)
  no operation moved by 1% of the time
where the time goes in v7:
time: 44.4 us; the launch traced here: 44.3 us
  Pallas kernels  42.4 us (95%)
  local copies, waits for them, and re-layouts  1.25 us (3%)
  between operations  0.64 us (1%)
    pallas_call x1, Pallas kernels, per_device(): pl.pallas_call(functools.partial(kernel, na), out_shape=(vmem((n, WIDTH),...  42.4 us
    unnamed x2, local copies, waits for them, and re-layouts  1.25 us

profile of v7, /device:TPU:1, one launch (start us, length us, event | category | flops | bytes accessed | tf_op | source)
XLA Modules:
  0.0 44.3 jit_solution(18218686652091732369)
XLA Ops:
  0.6 42.4 %shard_map.122 = (bf16[128,256]{1,0:T(8,128)(2,1)S(1)}, bf16[1,128,128]{2,1,0:T(8,128)(2,1)S(1)}) custom-call(bf16[1,128,256]{2,1,0:T(8,128)(2,1)} %lineup.1, s32[1,128]{1,0:T(1,128)} %flags.1, bf16[1,128,128]{2,1,0:T(8,128)(2,1)} %couple.1, bf16[8,128]{1,0:T(8,128)(2,1)} %bitcast.7, bf16[256,1024]{1,0:T(8,128)(2,1)} %w_row.1, bf16[256,256]{1,0:T(8,128)(2,1)} %w_row_out.1, ...), custom_call_target="tpu_custom_call" | custom-call | tf_op jit(solution)/shard_map/pallas_call | solution.py:430
  43.0 0.6 %copy.15 = bf16[128,1,256]{2,0,1:T(8,128)(2,1)} copy(bf16[128,1,256]{2,0,1:T(8,128)(2,1)S(1)} %bitcast.4) | data formatting | bytes 131072
  43.6 0.6 %copy.16 = bf16[1,128,128]{2,1,0:T(8,128)(2,1)} copy(bf16[1,128,128]{2,1,0:T(8,128)(2,1)S(1)} %get-tuple-element.7) | data formatting | bytes 65536

commit v8 on v6

--- a/solution.py
+++ b/solution.py
@@ -363,10 +363,10 @@
         right_buf[y * NZ + k] = outer[OUTER:, k * n : (k + 1) * n]
     left_buf[b] = left_v[z]
     rights = right_buf.at[pl.ds(y * NZ, NZ)]
+    for r in b_far:
+        send(left_buf.at[b], left_buf.at[b], 5, a * NB + b_mate(r))
     for r in y_far:
         send(rights, rights, 6, a_mate(r) * NB + b)
-    for r in b_far:
-        send(left_buf.at[b], left_buf.at[b], 5, a * NB + b_mate(r))
     align_v[...] = updated.reshape(NZ, n, WIDTH)
     align_out[...] = align_v[z]
     wide[...] = couple_v[...].astype(F32)

time: 44.4 us -> 44.5 us (level)
  no operation moved by 1% of the time
where the time goes in v8:
time: 44.5 us; the launch traced here: 44.3 us
  Pallas kernels  42.4 us (95%)
  local copies, waits for them, and re-layouts  1.25 us (3%)
  between operations  0.64 us (1%)
    pallas_call x1, Pallas kernels, per_device(): pl.pallas_call(functools.partial(kernel, na), out_shape=(vmem((n, WIDTH),...  42.4 us
    unnamed x2, local copies, waits for them, and re-layouts  1.25 us

profile of v8, /device:TPU:1, one launch (start us, length us, event | category | flops | bytes accessed | tf_op | source)
XLA Modules:
  0.0 44.3 jit_solution(3217981772399906143)
XLA Ops:
  0.6 42.4 %shard_map.122 = (bf16[128,256]{1,0:T(8,128)(2,1)S(1)}, bf16[1,128,128]{2,1,0:T(8,128)(2,1)S(1)}) custom-call(bf16[1,128,256]{2,1,0:T(8,128)(2,1)} %lineup.1, s32[1,128]{1,0:T(1,128)} %flags.1, bf16[1,128,128]{2,1,0:T(8,128)(2,1)} %couple.1, bf16[8,128]{1,0:T(8,128)(2,1)} %bitcast.7, bf16[256,1024]{1,0:T(8,128)(2,1)} %w_row.1, bf16[256,256]{1,0:T(8,128)(2,1)} %w_row_out.1, ...), custom_call_target="tpu_custom_call" | custom-call | tf_op jit(solution)/shard_map/pallas_call | solution.py:430
  43.0 0.6 %copy.15 = bf16[128,1,256]{2,0,1:T(8,128)(2,1)} copy(bf16[128,1,256]{2,0,1:T(8,128)(2,1)S(1)} %bitcast.4) | data formatting | bytes 131072
  43.7 0.6 %copy.16 = bf16[1,128,128]{2,1,0:T(8,128)(2,1)} copy(bf16[1,128,128]{2,1,0:T(8,128)(2,1)S(1)} %get-tuple-element.7) | data formatting | bytes 65536
